TPU v7x, 128 devices: a whole 4x4x4 slice. The times are simulated.
128 devices in a mesh: pts: 64 (over x, y, z), grp: 2 (over core).
Axes of the slice: x: 4, y: 4, z: 4, core: 2. Of those that a mesh axis runs over, the one named last changes fastest.
Arguments:
- mesh_samples: bfloat16 [1048576, 256], P(('pts', 'grp')), may hold values from -6 to 6
- upstream_derivative: bfloat16 [1048576, 256], P(('pts', 'grp')), may hold values from -6 to 6
- group_skin_region: int32 [64, 2, 16], replicated, may hold values from 0 to 511
- chip_group_tally: int32 [64, 2], replicated, may hold values from 1 to 16, as said below
- region_vector_lookup: bfloat16 [512, 256], replicated, may hold values from -3 to 3
- entry_matrix: bfloat16 [256, 512], replicated, may hold values from -0.375 to 0.375
- partition_matrix: bfloat16 [32, 64], replicated, may hold values from -1 to 1
- softmax_sharpness: float32 [8], replicated, may hold values from 0.25 to 2
- triple_mapping_matrix: bfloat16 [32, 96], replicated, may hold values from -1 to 1
- exit_matrix: bfloat16 [256, 256], replicated, may hold values from -0.375 to 0.375
Outputs:
- grad_points: bfloat16 [1048576, 256], P(('pts', 'grp'))
- grad_patch: float32 [512, 256], replicated
- grad_w_in: float32 [256, 512], replicated
- grad_w_slice: float32 [32, 64], replicated
- grad_temperature: float32 [8], replicated
- grad_w_qkv: float32 [32, 96], replicated
- grad_w_out: float32 [256, 256], replicated
Inputs may be any that keep to these rules, and one draw needn't show every extreme that they name: `chip_group_tally`: the points of a device fill its first row blocks; in every draw some device holds 16 blocks.
All inputs are finite; a program needn't handle non-finite values.
Results may differ from a plain program's by a relative error of at most 0.012.
The roundings to bfloat16 on the way count: a program that leaves them out, or rounds other values in their place, can miss the bound.
Values may be sent and summed in bfloat16 or wider, within the bound.
No kernel may reach another device: no remote copies, remote signals or barrier semaphores. Data moves between devices by JAX's collectives and lax.ppermute only.
A program may use at most 192 MiB of HBM per device.

v0:
```python
import math

import jax
import jax.numpy as jnp
from jax import lax
from jax.sharding import PartitionSpec as P

BLOCK_ROWS = 512


EPS = 1e-05
HIGH = lax.Precision.HIGHEST


def attend(token, w_qkv_f):
    head_dim = token.shape[-1]
    qkv = jnp.einsum("hgd,de->hge", token, w_qkv_f, precision=HIGH)
    query = qkv[..., :head_dim]
    keys = qkv[..., head_dim : 2 * head_dim]
    values = qkv[..., 2 * head_dim :]
    scores = jnp.einsum("hgd,hkd->hgk", query, keys, precision=HIGH) / math.sqrt(head_dim)
    probs = jax.nn.softmax(scores, axis=-1)
    return jnp.einsum("hgk,hkd->hgd", probs, values, precision=HIGH)


def slice_middle(norm, raw, grad_otb, triple_mapping_matrix):
    denom = norm + EPS
    token = raw / denom[..., None]
    out_tok, pullback = jax.vjp(attend, token, triple_mapping_matrix.astype(jnp.float32))
    grad_token, derivative_triple_matrix = pullback(grad_otb)
    unnormalized_gradient = (grad_token / denom[..., None]).astype(jnp.bfloat16)
    gradient_of_norm = -jnp.sum(grad_token * token, axis=-1) / denom
    return (
        out_tok.astype(jnp.bfloat16),
        unnormalized_gradient,
        gradient_of_norm,
        derivative_triple_matrix,
    )


def partition_raw_affinity(mapped_source, partition_matrix, softmax_sharpness):
    rows = mapped_source.shape[0]
    channel_divided_lines = softmax_sharpness.shape[0]
    width = mapped_source.shape[1] // 2
    hidden_activations = mapped_source[:, :width].reshape(
        rows, channel_divided_lines, width // channel_divided_lines
    )
    membership_raw_scores = jnp.einsum(
        "xzm,mg->xzg", hidden_activations, partition_matrix, preferred_element_type=jnp.float32
    )
    return membership_raw_scores / softmax_sharpness[None, :, None]


def make_input(x_rows, patch_id, region_vector_lookup):
    patch_row = lax.dynamic_slice_in_dim(region_vector_lookup, patch_id, 1, 0)
    return (x_rows.astype(jnp.float32) + patch_row.astype(jnp.float32)).astype(jnp.bfloat16)


def grad_y_of(cotangent_row_values, exit_matrix, channel_divided_lines):
    rows = cotangent_row_values.shape[0]
    grad_y = lax.dot_general(
        cotangent_row_values,
        exit_matrix,
        (((1,), (1,)), ((), ())),
        preferred_element_type=jnp.float32,
    )
    return grad_y.astype(jnp.bfloat16).reshape(
        rows, channel_divided_lines, exit_matrix.shape[0] // channel_divided_lines
    )


def partial_sums(mapped_source, membership_raw_scores, cotangent_row_values, exit_matrix):
    rows, channel_divided_lines, slices = membership_raw_scores.shape
    width = mapped_source.shape[1] // 2
    weights = jax.nn.softmax(membership_raw_scores, axis=-1)
    weights_b = weights.astype(jnp.bfloat16)
    fx = mapped_source[:, width:].reshape(
        rows, channel_divided_lines, width // channel_divided_lines
    )
    grad_y = grad_y_of(cotangent_row_values, exit_matrix, channel_divided_lines)
    raw = jnp.einsum("rhg,rhd->hgd", weights_b, fx, preferred_element_type=jnp.float32)
    gsum = jnp.einsum("rhg,rhd->hgd", weights_b, grad_y, preferred_element_type=jnp.float32)
    return (jnp.sum(weights, axis=0), raw, gsum)


def reverse_sweep_lines(
    input_points,
    mapped_source,
    membership_raw_scores,
    cotangent_row_values,
    output_bias_rows,
    unnormalized_gradient,
    gradient_of_norm,
    entry_matrix,
    partition_matrix,
    softmax_sharpness,
    exit_matrix,
):
    rows = input_points.shape[0]
    channel_divided_lines, slices, head_dim = output_bias_rows.shape
    width = channel_divided_lines * head_dim
    weights = jax.nn.softmax(membership_raw_scores, axis=-1)
    weights_b = weights.astype(jnp.bfloat16)
    hidden_activations = mapped_source[:, :width].reshape(rows, channel_divided_lines, head_dim)
    fx = mapped_source[:, width:].reshape(rows, channel_divided_lines, head_dim)
    mixed = jnp.einsum(
        "rhg,hgd->rhd", weights_b, output_bias_rows, preferred_element_type=jnp.float32
    )
    mixed = mixed.astype(jnp.bfloat16).reshape(rows, width)
    derivative_leaving = lax.dot_general(
        mixed, cotangent_row_values, (((0,), (0,)), ((), ())), preferred_element_type=jnp.float32
    )
    grad_y = grad_y_of(cotangent_row_values, exit_matrix, channel_divided_lines)
    grad_w = jnp.einsum(
        "rhd,hgd->rhg", grad_y, output_bias_rows, preferred_element_type=jnp.float32
    )
    grad_w = (
        grad_w
        + jnp.einsum("rhd,hgd->rhg", fx, unnormalized_gradient, preferred_element_type=jnp.float32)
        + gradient_of_norm[None]
    )
    derivative_raw_membership = weights * (
        grad_w - jnp.sum(weights * grad_w, axis=-1, keepdims=True)
    )
    sharpness_derivative = (
        -jnp.sum(derivative_raw_membership * membership_raw_scores, axis=(0, 2)) / softmax_sharpness
    )
    partition_derivative = (derivative_raw_membership / softmax_sharpness[None, :, None]).astype(
        jnp.bfloat16
    )
    derivative_partition = jnp.einsum(
        "rhd,rhg->dg", hidden_activations, partition_derivative, preferred_element_type=jnp.float32
    )
    grad_mid = jnp.einsum(
        "rhg,dg->rhd", partition_derivative, partition_matrix, preferred_element_type=jnp.float32
    )
    grad_fx = jnp.einsum(
        "rhg,hgd->rhd", weights_b, unnormalized_gradient, preferred_element_type=jnp.float32
    )
    grad_proj = jnp.concatenate(
        [grad_mid.reshape(rows, width), grad_fx.reshape(rows, width)], axis=1
    ).astype(jnp.bfloat16)
    derivative_entering = lax.dot_general(
        input_points, grad_proj, (((0,), (0,)), ((), ())), preferred_element_type=jnp.float32
    )
    derivative_layer_source = lax.dot_general(
        grad_proj, entry_matrix, (((1,), (1,)), ((), ())), preferred_element_type=jnp.float32
    )
    return (
        derivative_entering,
        derivative_leaving,
        derivative_partition,
        sharpness_derivative,
        derivative_layer_source,
    )


def shards(
    mesh_samples,
    upstream_derivative,
    group_skin_region,
    chip_group_tally,
    region_vector_lookup,
    entry_matrix,
    partition_matrix,
    softmax_sharpness,
    triple_mapping_matrix,
    exit_matrix,
):
    width = entry_matrix.shape[0]
    channel_divided_lines = softmax_sharpness.shape[0]
    slices = partition_matrix.shape[1]
    head_dim = width // channel_divided_lines
    patches_all = region_vector_lookup.shape[0]
    pts_pos = lax.axis_index("pts")
    grp_pos = lax.axis_index("grp")
    own_count = chip_group_tally[pts_pos, grp_pos]
    patch_ids = group_skin_region[pts_pos, grp_pos]
    first = jnp.int32(0)
    rows_total = mesh_samples.shape[0]

    def locate(step):
        slot = jnp.where(step < own_count, step, step)
        patch_slot = jnp.where(step < own_count, step, step)
        row_start = slot * BLOCK_ROWS
        x_rows = lax.dynamic_slice_in_dim(mesh_samples, row_start, BLOCK_ROWS, 0)
        cotangent_row_values = lax.dynamic_slice_in_dim(
            upstream_derivative, row_start, BLOCK_ROWS, 0
        )
        return (row_start, x_rows, cotangent_row_values, patch_ids[patch_slot])

    zero_sums = (
        jnp.zeros((channel_divided_lines, slices), jnp.float32),
        jnp.zeros((channel_divided_lines, slices, head_dim), jnp.float32),
        jnp.zeros((channel_divided_lines, slices, head_dim), jnp.float32),
    )

    def first_kept(step, running_state):
        sums, kept_proj, kept_logits = running_state
        row_start, x_rows, cotangent_row_values, patch_id = locate(step)
        input_points = make_input(x_rows, patch_id, region_vector_lookup)
        mapped_source = jnp.dot(
            input_points, entry_matrix, preferred_element_type=jnp.float32
        ).astype(jnp.bfloat16)
        membership_raw_scores = partition_raw_affinity(
            mapped_source, partition_matrix, softmax_sharpness
        )
        part = partial_sums(mapped_source, membership_raw_scores, cotangent_row_values, exit_matrix)
        sums = (sums[0] + part[0], sums[1] + part[1], sums[2] + part[2])
        kept_proj = lax.dynamic_update_slice_in_dim(kept_proj, mapped_source, row_start, 0)
        kept_logits = lax.dynamic_update_slice_in_dim(
            kept_logits,
            membership_raw_scores.reshape(BLOCK_ROWS, channel_divided_lines * slices),
            row_start,
            0,
        )
        return (sums, kept_proj, kept_logits)

    start_state = (
        zero_sums,
        jnp.zeros((rows_total, 2 * width), jnp.bfloat16),
        jnp.zeros((rows_total, channel_divided_lines * slices), jnp.float32),
    )
    sums, kept_proj, kept_logits = lax.fori_loop(first, own_count, first_kept, start_state)

    def recall(row_start):
        mapped_source = lax.dynamic_slice_in_dim(kept_proj, row_start, BLOCK_ROWS, 0)
        membership_raw_scores = lax.dynamic_slice_in_dim(kept_logits, row_start, BLOCK_ROWS, 0)
        return (
            mapped_source,
            membership_raw_scores.reshape(BLOCK_ROWS, channel_divided_lines, slices),
        )

    norm, raw, grad_otb = lax.psum((sums[0], sums[1], sums[2]), ("pts", "grp"))
    output_bias_rows, unnormalized_gradient, gradient_of_norm, derivative_triple_matrix = (
        slice_middle(norm, raw, grad_otb, triple_mapping_matrix)
    )
    patch_range = jnp.arange(patches_all, dtype=jnp.int32)

    def second_step(step, running_state):
        parameter_derivatives, derivative_storage = running_state
        row_start, x_rows, cotangent_row_values, patch_id = locate(step)
        input_points = make_input(x_rows, patch_id, region_vector_lookup)
        mapped_source, membership_raw_scores = recall(row_start)
        (
            derivative_entering,
            derivative_leaving,
            derivative_partition,
            sharpness_derivative,
            derivative_layer_source,
        ) = reverse_sweep_lines(
            input_points,
            mapped_source,
            membership_raw_scores,
            cotangent_row_values,
            output_bias_rows,
            unnormalized_gradient,
            gradient_of_norm,
            entry_matrix,
            partition_matrix,
            softmax_sharpness,
            exit_matrix,
        )
        patch_mask = (patch_range == patch_id).astype(jnp.float32)
        derivative_region = patch_mask[:, None] * jnp.sum(derivative_layer_source, axis=0)[None, :]
        parameter_derivatives = (
            parameter_derivatives[0] + derivative_entering,
            parameter_derivatives[1] + derivative_leaving,
            parameter_derivatives[2] + derivative_partition,
            parameter_derivatives[3] + sharpness_derivative,
            parameter_derivatives[4] + derivative_region,
        )
        derivative_storage = lax.dynamic_update_slice_in_dim(
            derivative_storage, derivative_layer_source.astype(jnp.bfloat16), row_start, 0
        )
        return (parameter_derivatives, derivative_storage)

    zero_grads = (
        jnp.zeros((width, 2 * width), jnp.float32),
        jnp.zeros((width, width), jnp.float32),
        jnp.zeros((head_dim, slices), jnp.float32),
        jnp.zeros((channel_divided_lines,), jnp.float32),
        jnp.zeros((patches_all, width), jnp.float32),
    )
    parameter_derivatives, derivative_storage = lax.fori_loop(
        first, own_count, second_step, (zero_grads, jnp.zeros((rows_total, width), jnp.bfloat16))
    )
    (
        derivative_entering,
        derivative_leaving,
        derivative_partition,
        sharpness_derivative,
        derivative_region,
    ) = lax.psum(
        (
            parameter_derivatives[0],
            parameter_derivatives[1],
            parameter_derivatives[2],
            parameter_derivatives[3],
            parameter_derivatives[4],
        ),
        ("pts", "grp"),
    )
    return (
        derivative_storage,
        derivative_region,
        derivative_entering,
        derivative_partition,
        sharpness_derivative,
        derivative_triple_matrix,
        derivative_leaving,
    )


def solution(mesh):
    in_specs = (
        P(("pts", "grp"), None),
        P(("pts", "grp"), None),
        P(),
        P(),
        P(),
        P(),
        P(),
        P(),
        P(),
        P(),
    )
    out_specs = (P(("pts", "grp"), None), P(), P(), P(), P(), P(), P())
    return jax.shard_map(shards, mesh=mesh, in_specs=in_specs, out_specs=out_specs, check_vma=False)
```

profile of v0, /device:TPU:1, one launch (start us, length us, event | category | flops | bytes accessed | tf_op | source)
XLA Modules:
  0.0 986.7 jit_solution(41139169403122783)
XLA Ops:
  8.8 7.8 broadcast_in_dim.51
  16.5 4.2 broadcast_in_dim.50
  20.9 184.8 %while.39 = (s32[]{:T(128)}, f32[8,64]{1,0:T(8,128)S(1)}, f32[8,64,32]{1,2,0:T(8,128)S(1)}, f32[8,64,32]{1,2,0:T(8,128)S(1)}, bf16[8192,512]{0,1:T(8,128)(2,1)},...) while((s32[]{:T(128)}, f32[8,64]{1,0:T(8,128)S(1)}, ...), condition=%wide.region_4.5_spmd, body=%wide.region_0.4_spmd.sunk | while | flops 271876416 | bytes 12013439 | solution.py:224
  24.8 2.3 constant_dynamic-update-slice_fusion.4
  36.4 2.2 constant_dynamic-update-slice_fusion.4
  47.9 2.2 constant_dynamic-update-slice_fusion.4
  59.4 2.3 constant_dynamic-update-slice_fusion.4
  71.0 2.2 constant_dynamic-update-slice_fusion.4
  82.5 2.3 constant_dynamic-update-slice_fusion.4
  94.0 2.3 constant_dynamic-update-slice_fusion.4
  105.6 2.2 constant_dynamic-update-slice_fusion.4
  117.1 2.2 constant_dynamic-update-slice_fusion.4
  128.6 2.2 constant_dynamic-update-slice_fusion.4
  140.0 2.2 constant_dynamic-update-slice_fusion.4
  151.5 2.2 constant_dynamic-update-slice_fusion.4
  162.9 2.2 constant_dynamic-update-slice_fusion.4
  174.4 2.2 constant_dynamic-update-slice_fusion.4
  185.9 2.2 constant_dynamic-update-slice_fusion.4
  197.4 2.2 constant_dynamic-update-slice_fusion.4
  206.4 69.0 %psum.57 = f32[8,64]{1,0:T(8,128)S(1)} all-reduce(f32[8,64]{1,0:T(8,128)S(1)} %get-tuple-element.209), channel_id=1, replica_groups=mesh['pts'=64,'grp'=2] {'pts','grp'}, use_global_device_ids=true, to_apply=%region_6.7 | all-reduce | flops 512 | bytes 4096 | tf_op jit(solution)/shard_map/psum | solution.py:234
  275.4 75.9 %all-reduce.11.cloned.1.call-done = (f32[8,64,32]{1,2,0:T(8,128)}, f32[8,64,32]{1,2,0:T(8,128)}) async-done(((f32[8,64,32]{1,2,0:T(8,128)}, f32[8,64,32]{1,2,0:T(8,128)}), (f32[8,64,32]{1,2,0:T(8,128)}, f32[8,64,32]{1,2,0:T(8,128)})) %all-reduce.11.cloned.1.call-update) | async-done | bytes 131088 | tf_op jit(solution)/shard_map/psum | solution.py:234
  360.4 2.3 broadcast_in_dim.48
  365.5 462.1 %while.40 = (s32[]{:T(128)}, f32[256,512]{1,0:T(8,128)}, f32[256,256]{1,0:T(8,128)S(1)}, f32[32,64]{1,0:T(8,128)}, f32[8]{0:T(128)}, /*index=5*/f32[512,256]{1,0...) while((s32[]{:T(128)}, f32[256,512]{1,0:T(8,128)}, ...), condition=%wide.region_18.0_spmd.clone, body=%wide.region_12.18_spmd.clone.sunk | while | flops 512048416 | bytes 25329084 | solution.py:285
  377.7 2.0 fusion.176
  382.2 2.0 multiply_add_fusion.2
  386.8 2.4 convolution_add_fusion.11
  406.5 2.0 fusion.176
  411.1 2.0 multiply_add_fusion.2
  415.6 2.4 convolution_add_fusion.11
  435.3 2.0 fusion.176
  439.9 2.0 multiply_add_fusion.2
  444.4 2.4 convolution_add_fusion.11
  464.2 2.0 fusion.176
  468.7 2.0 multiply_add_fusion.2
  473.2 2.4 convolution_add_fusion.11
  493.0 2.0 fusion.176
  497.5 2.0 multiply_add_fusion.2
  502.1 2.4 convolution_add_fusion.11
  526.4 2.0 multiply_add_fusion.2
  530.9 2.4 convolution_add_fusion.11
  550.6 2.0 fusion.176
  555.2 2.0 multiply_add_fusion.2
  559.7 2.4 convolution_add_fusion.11
  584.0 2.0 multiply_add_fusion.2
  588.5 2.4 convolution_add_fusion.11
  612.8 2.0 multiply_add_fusion.2
  617.4 2.4 convolution_add_fusion.11
  641.7 2.0 multiply_add_fusion.2
  646.2 2.4 convolution_add_fusion.11
  670.5 2.0 multiply_add_fusion.2
  675.0 2.4 convolution_add_fusion.11
  699.3 2.0 multiply_add_fusion.2
  703.8 2.4 convolution_add_fusion.11
  728.1 2.0 multiply_add_fusion.2
  732.7 2.4 convolution_add_fusion.11
  757.0 2.0 multiply_add_fusion.2
  761.5 2.4 convolution_add_fusion.11
  785.8 2.0 multiply_add_fusion.2
  790.3 2.4 convolution_add_fusion.11
  814.6 2.0 multiply_add_fusion.2
  819.1 2.4 convolution_add_fusion.11
  828.3 63.9 %all-reduce.3 = (f32[32,64]{1,0:T(8,128)}, f32[8]{0:T(128)}) all-reduce(f32[32,64]{1,0:T(8,128)} %get-tuple-element.215, f32[8]{0:T(128)} %get-tuple-element.216), channel_id=1, replica_groups=mesh['pts'=64,'grp'=2] {'pts','grp'}, use_global_device_ids=true, to_apply=%region_21.22 | all-reduce | flops 2056 | bytes 16448 | tf_op jit(solution)/shard_map/psum | solution.py:294
  892.3 2.2 convolution_bitcast_fusion.1
  894.4 80.0 %all-reduce.9.cloned.1.call-done = (f32[512,256]{1,0:T(8,128)}, f32[256,512]{1,0:T(8,128)}, f32[256,256]{1,0:T(8,128)}) async-done(((f32[512,256]{1,0:T(8,128)}, f32[256,512]{1,0:T(8,128)}, f32[256,256]{1,0:T(8,128)}), (f32[512,256]{1,0:T(8,128)}, f32[256,512]{1,0:T(8,128)}, f32[256,256]{1,0:T(8,128)})) %all-reduce.9.cloned.1.call-update) | async-done | bytes 1310736 | tf_op jit(solution)/shard_map/psum | solution.py:294
  (626 shorter events, 462.6 us)
Async XLA Ops:
  7.2 1.4 copy-start
  7.2 344.1 %all-reduce.11.cloned.1.call-start = ((), (), s32[]{:S(2)}) async-start(), calls=%async_computation.1 | async-start | bytes 524288 | tf_op jit(solution)/shard_map/psum | solution.py:234
  16.5 4.3 copy-start.1
  16.5 4.3 copy-start.6
  20.8 330.5 %copy-start.12 = (bf16[32,96]{1,0:T(8,128)(2,1)S(1)}, bf16[32,96]{1,0:T(8,128)(2,1)}, u32[]{:S(2)}) copy-start(bf16[32,96]{1,0:T(8,128)(2,1)} %param.22) | copy-start | bytes 18436
  205.6 0.7 copy-start.3
  205.6 0.7 copy-start.4
  205.7 152.0 %copy-start.10 = (s32[16]{0:T(128)}, s32[16]{0:T(128)S(1)}, u32[]{:S(2)}) copy-start(s32[16]{0:T(128)S(1)} %get-tuple-element.790) | copy-start | bytes 196
  206.4 768.1 %all-reduce.9.cloned.1.call-start = ((), (), s32[]{:S(2)}) async-start(), calls=%async_computation | async-start | bytes 2621440 | tf_op jit(solution)/shard_map/psum | solution.py:294
  275.4 84.5 %copy-start.9 = (f32[8,64]{1,0:T(8,128)}, f32[8,64]{1,0:T(8,128)S(1)}, u32[]{:S(2)}) copy-start(f32[8,64]{1,0:T(8,128)S(1)} %broadcast_add_fusion) | copy-start | bytes 6148
  351.3 7.6 copy-start.11
  354.9 7.8 copy-start.15
  356.9 6.6 copy-start.13
  357.6 7.9 copy-start.14
  366.4 7.6 copy-start.7
  374.0 0.8 copy-start.5
  389.1 5.4 copy-start.8
  395.2 7.6 copy-start.7
  402.8 0.8 copy-start.5
  417.9 5.4 copy-start.8
  424.1 7.6 copy-start.7
  431.7 0.8 copy-start.5
  446.8 5.4 copy-start.8
  452.9 7.6 copy-start.7
  460.5 0.8 copy-start.5
  475.6 5.4 copy-start.8
  481.7 7.6 copy-start.7
  489.3 0.8 copy-start.5
  504.4 5.4 copy-start.8
  510.5 7.6 copy-start.7
  518.1 0.8 copy-start.5
  533.2 5.4 copy-start.8
  539.4 7.6 copy-start.7
  547.0 0.8 copy-start.5
  562.1 5.4 copy-start.8
  568.2 7.6 copy-start.7
  575.8 0.8 copy-start.5
  590.9 5.4 copy-start.8
  597.0 7.6 copy-start.7
  604.6 0.8 copy-start.5
  619.7 5.4 copy-start.8
  625.8 7.6 copy-start.7
  633.4 0.8 copy-start.5
  648.5 5.4 copy-start.8
  654.7 7.6 copy-start.7
  662.3 0.8 copy-start.5
  677.4 5.4 copy-start.8
  683.5 7.6 copy-start.7
  691.1 0.8 copy-start.5
  706.2 5.4 copy-start.8
  712.3 7.6 copy-start.7
  719.9 0.8 copy-start.5
  735.0 5.4 copy-start.8
  741.1 7.6 copy-start.7
  748.7 0.8 copy-start.5
  763.8 5.4 copy-start.8
  770.0 7.6 copy-start.7
  777.6 0.8 copy-start.5
  792.7 5.4 copy-start.8
  798.8 7.6 copy-start.7
  806.4 0.8 copy-start.5
  821.5 5.4 copy-start.8
  827.6 0.7 copy-start.2
Sparse Core Ops, SparseCore 0:
  206.5 144.8 all-reduce.10
  828.5 145.9 all-reduce.8
where the time goes:
time: 999 us; the launch traced here: 987 us
  matrix products  348 us (35%)
  waiting for transfers between devices  156 us (16%)
  blocking collectives  133 us (13%)
  other arithmetic  126 us (13%)
  local copies, waits for them, and re-layouts  122 us (12%)
  loops' own time  87.7 us (9%)
  between operations  14.2 us (1%)
    psum x1, waiting for transfers between devices, shards(): lax.psum((parameter_derivatives[0], parameter_derivatives[1], parameter_d...  80 us
    psum x1, waiting for transfers between devices, shards(): norm, raw, grad_otb = lax.psum((sums[0], sums[1], sums[2]), ('pts', 'grp'))  75.9 us
    psum x1, blocking collectives, shards(): norm, raw, grad_otb = lax.psum((sums[0], sums[1], sums[2]), ('pts', 'grp'))  69 us
    psum x1, blocking collectives, shards(): lax.psum((parameter_derivatives[0], parameter_derivatives[1], parameter_d...  63.9 us
    another operation x1, loops' own time, shards(): lax.fori_loop(first, own_count, first_kept, start_state)  44 us
    another operation x1, loops' own time, shards(): lax.fori_loop(first, own_count, second_step, (zero_grads, jnp.zeros((rows...  43.8 us
    dot_general x32, matrix products, grad_y_of(): lax.dot_general(cotangent_row_values, exit_matrix, (((1,), (1,)), ((), ()...  38.9 us
    dot_general x16, matrix products, reverse_sweep_lines(): lax.dot_general(input_points, grad_proj, (((0,), (0,)), ((), ())), prefer...  37.6 us
  transfers between devices with their start and end apart: 2, of which 2 were waited for; matrix products, arithmetic and copies ran while one was open for 0% of the time, Pallas kernels for 0%

commit v1 on v0

v1 whole, which is shorter than its diff:
```python
import functools
import math

import jax
import jax.numpy as jnp
from jax import lax
from jax.experimental import pallas as pl
from jax.experimental.pallas import tpu as pltpu
from jax.sharding import PartitionSpec as P

f32 = jnp.float32
bf16 = jnp.bfloat16
HIGH = lax.Precision.HIGHEST
EPS = 1e-05
LOG2E = math.log2(math.e)

ROWS = 512
BLOCKS = 16
STEP = 1024
STEPS = BLOCKS * ROWS // STEP
C = 256
H = 8
D = 32
G = 64
HG = H * G
PATCHES = 512
SUMS = 136
MID = 224
PIECE = 176
HALF = 4 * PIECE
BUF = 2 * HALF
VMEM_LIMIT = 24 * 2**20
SMALL = pltpu.CompilerParams(vmem_limit_bytes=8 * 2**20)

NN = (((1,), (0,)), ((), ()))
NT = (((1,), (1,)), ((), ()))
TN = (((0,), (0,)), ((), ()))


def dot(a, b, dims, precision=None):
    return lax.dot_general(a, b, dims, precision=precision, preferred_element_type=f32)


def split(a):
    hi = a.astype(bf16)
    return hi, (a - hi.astype(f32)).astype(bf16)


def dot_left2(a, b, dims):
    hi, lo = split(a)
    return dot(hi, b, dims) + dot(lo, b, dims)


def dot_right2(a, b, dims):
    hi, lo = split(b)
    return dot(a, hi, dims) + dot(a, lo, dims)


def iota(shape, dim):
    return lax.broadcasted_iota(jnp.int32, shape, dim)


def head_mask(j, rows):
    return (iota((rows, 128), 1) >> 5) == j


def spread(packed):
    return jnp.concatenate([jnp.where(head_mask(j, G), packed, 0.0) for j in range(4)], axis=0)


def gather_heads(wide):
    total = jnp.where(head_mask(0, G), wide[0:G], 0.0)
    for j in range(1, 4):
        total = total + jnp.where(head_mask(j, G), wide[j * G : (j + 1) * G], 0.0)
    return total


def in_vmem():
    return pl.BlockSpec(memory_space=pltpu.VMEM)


def in_smem():
    return pl.BlockSpec(memory_space=pltpu.SMEM)


def in_hbm():
    return pl.BlockSpec(memory_space=pl.ANY)


def hbm(v):
    return pltpu.with_memory_space_constraint(v, pltpu.HBM)


def vmem(v):
    return pltpu.with_memory_space_constraint(v, pltpu.VMEM)


def place():
    return lax.axis_index("pts"), lax.axis_index("grp")


def block_count(tally_ref):
    pts, grp = place()
    return tally_ref[pts, grp]


def patch_onehot(region_ref):
    pts, grp = place()
    ids = region_ref[pts, pl.ds(grp, 1), :]
    return (iota((PATCHES, BLOCKS), 0) == ids).astype(f32)


def add_block_sums(ref, at, wide, b):
    lane = iota((G, 128), 1)
    old = ref[at, :]
    for k in range(2):
        lo = k * ROWS
        part = (wide[:, lo : lo + 128] + wide[:, lo + 128 : lo + 256]) + (
            wide[:, lo + 256 : lo + 384] + wide[:, lo + 384 : lo + 512]
        )
        old = jnp.where(lane == 2 * b + k, jnp.sum(part, axis=1, keepdims=True), old)
    ref[at, :] = old


def first_kernel(
    tally_ref,
    region_ref,
    temp_ref,
    x_hbm,
    u_hbm,
    lut_hbm,
    e_in_hbm,
    x_out_hbm,
    p_hbm,
    w_ref,
    fg_ref,
    xin_ref,
    u_ref,
    keep_ref,
    send_ref,
    cw_ref,
    pblk_ref,
    x_ref,
    lut_ref,
    e_in_ref,
    x_out_ref,
    p_ref,
    et_ref,
    rows_ref,
    acc_ref,
    x_sem,
    u_sem,
    sem,
):
    count = block_count(tally_ref)
    steps = (count + 1) >> 1
    small = [
        pltpu.make_async_copy(src, dst, sem.at[k])
        for k, (src, dst) in enumerate(
            (
                (e_in_hbm, e_in_ref),
                (p_hbm, p_ref),
                (lut_hbm, lut_ref),
                (x_out_hbm, x_out_ref),
            )
        )
    ]
    for copy in small:
        copy.start()

    def rows_copies(b):
        at = pl.ds(pl.multiple_of(b * STEP, STEP), STEP)
        return (
            pltpu.make_async_copy(x_hbm.at[at, :], x_ref.at[b], x_sem.at[b]),
            pltpu.make_async_copy(u_hbm.at[at, :], u_ref.at[b], u_sem.at[b]),
        )

    @pl.loop(0, steps)
    def _(b):
        for copy in rows_copies(b):
            copy.start()

    acc_ref[...] = jnp.zeros_like(acc_ref)
    cw_ref[...] = jnp.zeros_like(cw_ref)
    onehot = patch_onehot(region_ref).T.astype(bf16)
    for copy in small:
        copy.wait()
    et_ref[...] = e_in_ref[...].T
    t1 = ((iota((HG, G), 0) & (G - 1)) == iota((HG, G), 1)).astype(f32).astype(bf16)
    t2 = (iota((D, C), 0) == (iota((D, C), 1) & (D - 1))).astype(f32).astype(bf16)
    tall = dot(t1, p_ref[...], NT).astype(bf16)
    tiled = dot(tall, t2, NN)
    own = (iota((HG, C), 0) >> 6) == (iota((HG, C), 1) >> 5)
    pblk_ref[...] = jnp.where(own, tiled, 0.0).astype(bf16)
    rows_ref[...] = dot(onehot, lut_ref[...], NN)

    @pl.loop(0, steps)
    def _(b):
        for copy in rows_copies(b):
            copy.wait()
        for k in range(2):
            half = pl.ds(k * ROWS, ROWS)
            xin_ref[b, half, :] = (
                x_ref[b, half, :].astype(f32) + rows_ref[pl.ds(2 * b + k, 1), :]
            ).astype(bf16)
        proj = dot(et_ref[...], xin_ref[b], NT).astype(bf16)
        grad_y = dot(x_out_ref[...], u_ref[b], NT).astype(bf16)
        for q in range(2):
            fg_ref[b, 256 * q : 256 * q + 128, :] = proj[256 + 128 * q : 384 + 128 * q]
            fg_ref[b, 256 * q + 128 : 256 * q + 256, :] = grad_y[128 * q : 128 * q + 128]
        logits = dot(pblk_ref[...], proj[0:C], NN)
        valid = (iota((1, STEP), 1) + b * STEP < count * ROWS).astype(f32)
        for h in range(H):
            at = pl.ds(h * G, G)
            part = logits[G * h : G * h + G]
            scale = LOG2E / jnp.full((1, STEP), temp_ref[h], f32)
            top = jnp.max(part, axis=0, keepdims=True)
            ex = jnp.exp2((part - top) * scale)
            wt = ex * (valid / jnp.sum(ex, axis=0, keepdims=True))
            add_block_sums(cw_ref, at, wt, b)
            w_ref[b, at, :] = wt.astype(bf16)
        for q in range(2):
            at = pl.ds(256 * q, 256)
            acc_ref[q] += dot(w_ref[b, at, :], fg_ref[b, at, :], NT)

    core = lax.axis_index("grp")
    ones = jnp.ones((8, 128), f32)
    for q in range(2):
        raw = gather_heads(acc_ref[q, :, 0:128])
        grad = gather_heads(acc_ref[q, :, 128:256])
        norm = dot(ones, cw_ref[256 * q : 256 * q + 256, :], NT, HIGH)
        row = iota((8, 128), 0)
        norm = jnp.where(row == 0, norm[:, 0:128], jnp.where(row == 1, norm[:, 128:256], 0.0))

        def put(ref):
            ref[0:64, :] = raw
            ref[64:128, :] = grad
            ref[128:136, :] = norm

        pl.when(core == q)(lambda: put(keep_ref))
        pl.when(core != q)(lambda: put(send_ref))


def first_sweep(x, u, region, tally, lut, e_in, x_out, part, temp):
    return pl.pallas_call(
        first_kernel,
        in_specs=[in_smem(), in_vmem(), in_smem()] + [in_hbm()] * 6,
        out_specs=[in_vmem()] * 8,
        scratch_shapes=[
            pltpu.VMEM((STEPS, STEP, C), bf16),
            pltpu.VMEM((PATCHES, C), bf16),
            pltpu.VMEM((C, 2 * C), bf16),
            pltpu.VMEM((C, C), bf16),
            pltpu.VMEM((D, G), bf16),
            pltpu.VMEM((2 * C, C), bf16),
            pltpu.VMEM((BLOCKS, C), f32),
            pltpu.VMEM((2, 256, 256), f32),
            pltpu.SemaphoreType.DMA((STEPS,)),
            pltpu.SemaphoreType.DMA((STEPS,)),
            pltpu.SemaphoreType.DMA((4,)),
        ],
        out_shape=[
            pltpu.VMEM((STEPS, HG, STEP), bf16),
            pltpu.VMEM((STEPS, HG, STEP), bf16),
            pltpu.VMEM((STEPS, STEP, C), bf16),
            pltpu.VMEM((STEPS, STEP, C), bf16),
            jax.ShapeDtypeStruct((SUMS, 128), f32),
            jax.ShapeDtypeStruct((SUMS, 128), f32),
            jax.ShapeDtypeStruct((HG, 128), f32),
            jax.ShapeDtypeStruct((HG, C), bf16),
        ],
        compiler_params=pltpu.CompilerParams(vmem_limit_bytes=VMEM_LIMIT),
        name="first_sweep",
    )(tally, region, temp, *map(hbm, (x, u, lut, e_in, x_out, part)))


def moment_kernel(tally_ref, rows_ref, w_ref, y_ref):
    y_ref[...] = jnp.zeros_like(y_ref)

    @pl.loop(0, (block_count(tally_ref) + 1) >> 1)
    def _(b):
        y_ref[...] += dot(w_ref[b], rows_ref[b], NN)


def moment(name, tally, rows, w):
    return pl.pallas_call(
        moment_kernel,
        in_specs=[in_smem(), in_vmem(), in_vmem()],
        out_specs=in_vmem(),
        out_shape=jax.ShapeDtypeStruct((HG, C), f32),
        compiler_params=SMALL,
        cost_estimate=pl.CostEstimate(
            flops=2 * BLOCKS * ROWS * HG * C, bytes_accessed=8 * 2**20, transcendentals=0
        ),
        name=name,
    )(tally, vmem(rows), vmem(w))


def middle_kernel(s_ref, t_ref, out_ref):
    raw = s_ref[0:64, :]
    grad = s_ref[64:128, :]
    norm = jnp.concatenate([s_ref[128:136, :], jnp.zeros((120, 128), f32)], axis=0).T
    denom = jnp.full((G, 128), EPS, f32)
    for j in range(4):
        col = norm[G * (j % 2) : G * (j % 2) + G, j // 2 : j // 2 + 1]
        denom = denom + jnp.where(head_mask(j, G), col, 0.0)
    inv = 1.0 / denom
    token = raw * inv
    t2 = (iota((D, 128), 0) == (iota((D, 128), 1) & (D - 1))).astype(f32)
    own = (iota((128, 128), 0) >> 5) == (iota((128, 128), 1) >> 5)
    triple = t_ref[...].astype(f32)

    def diagonal(k):
        wide = dot(triple[:, D * k : D * k + D], t2, NN, HIGH)
        return jnp.where(own, jnp.concatenate([wide] * 4, axis=0), 0.0)

    wq, wk, wv = diagonal(0), diagonal(1), diagonal(2)
    query = dot(token, wq, NN, HIGH)
    keys = dot(token, wk, NN, HIGH)
    values = dot(token, wv, NN, HIGH)
    rate = 1.0 / math.sqrt(D)
    query_s = spread(query)
    scores = dot(query_s, keys, NT, HIGH) * rate
    scores = jnp.exp(scores - jnp.max(scores, axis=1, keepdims=True))
    probs = scores / jnp.sum(scores, axis=1, keepdims=True)
    out = gather_heads(dot(probs, values, NN, HIGH))
    grad_s = spread(grad)
    d_values = dot(probs.T, grad_s, NN, HIGH)
    d_probs = dot(grad_s, values, NT, HIGH)
    d_scores = probs * (d_probs - jnp.sum(d_probs * probs, axis=1, keepdims=True)) * rate
    d_query = gather_heads(dot(d_scores, keys, NN, HIGH))
    d_keys = dot(d_scores.T, query_s, NN, HIGH)
    d_token = (
        dot(d_query, wq, NT, HIGH) + dot(d_keys, wk, NT, HIGH) + dot(d_values, wv, NT, HIGH)
    )
    grad_raw = d_token * inv
    group = ((iota((128, 128), 0) >> 5) == iota((128, 128), 1)).astype(f32)
    first = (iota((128, 128), 1) < 4).astype(f32)
    grad_norm = -dot(d_token * token * inv, group * first, NN, HIGH)
    out_ref[0:64, :] = out.astype(bf16).astype(f32)
    out_ref[64:128, :] = grad_raw.astype(bf16).astype(f32)
    out_ref[128:192, :] = grad_norm
    token_t = jnp.concatenate([token, jnp.zeros((64, 128), f32)], axis=0).T[:, 0:64]
    total = jnp.zeros((D, 128), f32)
    for k, d_part in enumerate((d_query, d_keys, d_values)):
        full = jnp.where(own, dot(token_t, d_part, NN, HIGH), 0.0)
        full = full[0:32] + full[32:64] + (full[64:96] + full[96:128])
        fold = ((iota((128, 128), 0) & (D - 1)) + D * k == iota((128, 128), 1)).astype(f32)
        total = total + dot(full, fold, NN, HIGH)
    out_ref[192:224, :] = total


def middle(sums, triple):
    return pl.pallas_call(
        middle_kernel,
        out_shape=jax.ShapeDtypeStruct((MID, 128), f32),
        compiler_params=SMALL,
        name="middle",
    )(sums, triple)


def second_kernel(
    tally_ref,
    region_ref,
    temp_ref,
    temp_row_ref,
    xin_ref,
    w_ref,
    fg_ref,
    mine_ref,
    theirs_ref,
    e_in_ref,
    pblk_ref,
    p_ref,
    cw_ref,
    y_ref,
    z_ref,
    gs_ref,
    pq_ref,
    keep_ref,
    send_ref,
    og_ref,
    gn_ref,
    v_ref,
    cg_ref,
    ob_ref,
    gr_ref,
    buf_ref,
):
    steps = (block_count(tally_ref) + 1) >> 1
    core = lax.axis_index("grp")

    def prologue():
        for q in range(2):
            at = pl.ds(256 * q, 256)
            mine = core == q
            out_b = jnp.where(mine, mine_ref[0:64, :], theirs_ref[0:64, :])
            grad_raw = jnp.where(mine, mine_ref[64:128, :], theirs_ref[64:128, :])
            grad_norm = jnp.where(mine, mine_ref[128:192, :], theirs_ref[128:192, :])
            grad_norm = grad_norm - jnp.mean(grad_norm, axis=0, keepdims=True)
            for j in range(4):
                gn_ref[pl.ds(256 * q + G * j, G), :] = jnp.broadcast_to(
                    grad_norm[:, j : j + 1], (G, 128)
                )
            cols = pl.ds(128 * q, 128)
            off = slice(0, 256) if q else slice(256, 512)
            zero = jnp.zeros((256, 128), bf16)
            ob_ref[at, cols] = spread(out_b).astype(bf16)
            gr_ref[at, cols] = spread(grad_raw).astype(bf16)
            ob_ref[off, cols] = zero
            gr_ref[off, cols] = zero
            og_ref[at, 0:128] = spread(
                grad_raw - jnp.mean(grad_raw, axis=0, keepdims=True)
            ).astype(bf16)
            og_ref[at, 128:256] = spread(
                out_b - jnp.mean(out_b, axis=0, keepdims=True)
            ).astype(bf16)
        v_ref[...] = jnp.zeros_like(v_ref)
        cg_ref[...] = jnp.zeros_like(cg_ref)

    prologue()

    @pl.loop(0, steps)
    def _(b):
        for q in range(2):
            at = pl.ds(256 * q, 256)
            grad_w = dot(og_ref[at, :], fg_ref[b, at, :], NN)
            for j in range(4):
                h = 4 * q + j
                at = pl.ds(h * G, G)
                col = gn_ref[at, :]
                wt = w_ref[b, at, :].astype(f32)
                gw = grad_w[G * j : G * j + G] + jnp.concatenate([col] * (STEP // 128), axis=1)
                wg = wt * gw
                inv = 1.0 / jnp.full((1, STEP), temp_ref[h], f32)
                gs = (wg - wt * jnp.sum(wg, axis=0, keepdims=True)) * inv
                add_block_sums(cg_ref, at, gs, b)
                gs_ref[b, at, :] = gs.astype(bf16)
        v_ref[...] += dot(gs_ref[b], xin_ref[b], NN)

    v = v_ref[...]
    v_hi, v_lo = split(v)
    pblk = pblk_ref[...]
    gr = gr_ref[...]
    pq_ref[:, 0:512] = dot(e_in_ref[:, 0:256], pblk, NT).astype(bf16)
    pq_ref[:, 512:1024] = dot(e_in_ref[:, 256:512], gr, NT).astype(bf16)
    buf_ref[0:256, :] = dot_left2(v.T, pblk, NN)
    buf_ref[256:512, :] = dot_left2(y_ref[...].T, gr, NN)
    buf_ref[512:768, :] = dot_right2(ob_ref[...].astype(f32).T.astype(bf16), z_ref[...], NN)
    onehot = patch_onehot(region_ref).astype(bf16)
    per_block = dot_left2(cg_ref[...].T, pq_ref[:, 0:512], NT)
    per_block = per_block + dot_left2(cw_ref[...].T, pq_ref[:, 512:1024], NT)
    buf_ref[768:1280, :] = dot_right2(onehot, per_block[0:BLOCKS], NN)
    et = e_in_ref[:, 0:256].T
    cross = dot(et, v_hi, NT) + dot(et, v_lo, NT)
    own = (iota((256, 512), 0) >> 5) == (iota((256, 512), 1) >> 6)
    cross = jnp.where(own, cross, 0.0)
    heads = cross[0:32]
    for k in range(1, 8):
        heads = heads + cross[32 * k : 32 * k + 32]
    fold = ((iota((HG, 128), 0) & (G - 1)) == iota((HG, 128), 1)).astype(f32)
    tile = (iota((G, HG), 0) == (iota((G, HG), 1) & (G - 1))).astype(f32).astype(bf16)
    by_head = ((iota((HG, 8), 0) >> 6) == iota((HG, 8), 1)).astype(f32)
    weighed = heads * dot(p_ref[...], tile, NN)
    weighed = jnp.broadcast_to(jnp.sum(weighed, axis=0, keepdims=True), (8, HG))
    sharp = -dot(weighed, by_head, NN, HIGH) / temp_row_ref[...]
    buf_ref[1280:BUF, :] = jnp.zeros((BUF - 1280, 256), f32)
    buf_ref[1280:1312, 0:128] = dot(heads, fold, NN, HIGH)
    buf_ref[1312:1320, 0:8] = sharp
    keep_ref[...] = buf_ref[pl.ds(pl.multiple_of(core * HALF, 16), HALF), :]
    send_ref[...] = buf_ref[
        pl.ds(pl.multiple_of((1 - core) * HALF, 16), HALF), :
    ].astype(bf16)


def second_sweep(tally, region, temp, xin, w, fg, mine, theirs, e_in, pblk, part, cw, y, z):
    return pl.pallas_call(
        second_kernel,
        in_specs=[in_smem(), in_vmem(), in_smem()] + [in_vmem()] * 12,
        out_specs=[in_vmem()] * 4,
        scratch_shapes=[
            pltpu.VMEM((HG, 256), bf16),
            pltpu.VMEM((HG, 128), f32),
            pltpu.VMEM((HG, C), f32),
            pltpu.VMEM((HG, 128), f32),
            pltpu.VMEM((HG, C), bf16),
            pltpu.VMEM((HG, C), bf16),
            pltpu.VMEM((BUF, C), f32),
        ],
        out_shape=[
            pltpu.VMEM((STEPS, HG, STEP), bf16),
            jax.ShapeDtypeStruct((C, 1024), bf16),
            jax.ShapeDtypeStruct((HALF, C), f32),
            jax.ShapeDtypeStruct((HALF, C), bf16),
        ],
        compiler_params=pltpu.CompilerParams(vmem_limit_bytes=VMEM_LIMIT),
        name="second_sweep",
    )(
        tally, region, temp, temp.reshape(1, H), vmem(xin), vmem(w), vmem(fg), mine, theirs,
        e_in, pblk, part, cw, y, z,
    )


def points_kernel(first, number, tally_ref, gs_ref, w_ref, pq_ref, *refs):
    out_hbm, out_ref, sem = refs[-3:]
    steps = (block_count(tally_ref) + 1) >> 1

    def copy(k):
        at = pl.ds(pl.multiple_of((first + k) * STEP, STEP), STEP)
        return pltpu.make_async_copy(out_ref.at[k], out_hbm.at[at, :], sem.at[k])

    @pl.loop(0, number)
    def _(k):
        b = first + k

        @pl.when(b < steps)
        def _():
            grad = dot(pq_ref[:, 0:512], gs_ref[b], NN) + dot(pq_ref[:, 512:1024], w_ref[b], NN)
            out_ref[k] = grad.T.astype(bf16)

        @pl.when(b >= steps)
        def _():
            out_ref[k] = jnp.zeros((STEP, C), bf16)

        copy(k).start()

    @pl.loop(0, number)
    def _(k):
        copy(k).wait()


def points(tally, gs, w, pq, first, number, into=None):
    more = () if into is None else (into,)
    return pl.pallas_call(
        functools.partial(points_kernel, first, number),
        in_specs=[in_smem(), in_vmem(), in_vmem(), in_vmem()] + [in_hbm()] * len(more),
        out_specs=in_hbm(),
        out_shape=pltpu.HBM((BLOCKS * ROWS, C), bf16),
        scratch_shapes=[pltpu.VMEM((number, STEP, C), bf16), pltpu.SemaphoreType.DMA((number,))],
        input_output_aliases={4: 0} if more else {},
        compiler_params=SMALL,
        cost_estimate=pl.CostEstimate(
            flops=4 * number * STEP * HG * C, bytes_accessed=number * 2**20, transcendentals=0
        ),
        name="points",
    )(tally, vmem(gs), vmem(w), pq, *map(hbm, more))


def pieces_kernel(keep_ref, recv_ref, own_ref, p1_ref, p2_ref, p3_ref):
    z = lax.axis_index("pts") & 3

    def piece(k):
        at = pl.ds(pl.multiple_of(((z + k) & 3) * PIECE, 16), PIECE)
        return keep_ref[at, :] + recv_ref[at, :].astype(f32)

    own_ref[...] = piece(0)
    p1_ref[...] = piece(1).astype(bf16)
    p2_ref[...] = piece(2).astype(bf16)
    p3_ref[...] = piece(3).astype(bf16)


def pieces(keep, recv):
    spec = in_vmem()
    return pl.pallas_call(
        pieces_kernel,
        in_specs=[spec, spec],
        out_specs=[spec] * 4,
        out_shape=[jax.ShapeDtypeStruct((PIECE, C), f32)]
        + [jax.ShapeDtypeStruct((PIECE, C), bf16)] * 3,
        compiler_params=SMALL,
        name="pieces",
    )(keep, recv)


def final_kernel(mine_ref, theirs_ref, patch_ref, win_ref, slice_ref, temp_ref, wout_ref, buf_ref):
    core = lax.axis_index("grp")
    z = lax.axis_index("pts") & 3
    for ref, half in ((mine_ref, core), (theirs_ref, 1 - core)):
        for k in range(4):
            at = pl.multiple_of(half * HALF + ((z - k) & 3) * PIECE, 16)
            buf_ref[pl.ds(at, PIECE), :] = ref[k]
    win_ref[:, 0:256] = buf_ref[0:256, :].astype(f32)
    win_ref[:, 256:512] = buf_ref[256:512, :].astype(f32)
    wout_ref[...] = buf_ref[512:768, :].astype(f32)
    patch_ref[...] = buf_ref[768:1280, :].astype(f32)
    slice_ref[...] = buf_ref[1280:1312, 0:64].astype(f32)
    temp_ref[...] = buf_ref[1312:1328, 0:8].astype(f32)[0:1, :]


def final(mine, theirs):
    spec = in_vmem()
    return pl.pallas_call(
        final_kernel,
        in_specs=[spec, spec],
        out_specs=[spec] * 5,
        out_shape=[
            jax.ShapeDtypeStruct((PATCHES, C), f32),
            jax.ShapeDtypeStruct((C, 2 * C), f32),
            jax.ShapeDtypeStruct((D, G), f32),
            jax.ShapeDtypeStruct((1, H), f32),
            jax.ShapeDtypeStruct((C, C), f32),
        ],
        scratch_shapes=[pltpu.VMEM((BUF, C), bf16)],
        compiler_params=SMALL,
        name="final",
    )(mine, theirs)


def shift_pairs(dim, k):
    unit = (16, 4, 1)[dim]
    pairs = []
    for p in range(64):
        at = (p // unit) % 4
        pairs.append((p, p + ((at + k) % 4 - at) * unit))
    return pairs


def shift(v, dim, k):
    return lax.ppermute(v, "pts", shift_pairs(dim, k))


def swap(v):
    return lax.ppermute(v, "grp", [(0, 1), (1, 0)])


def ring_sum(v, dim):
    one, three, two = shift(v, dim, 1), shift(v, dim, 3), shift(v, dim, 2)
    return (v + two) + (one + three)


def ring_sum_b(v, dim):
    sent = v.astype(bf16)
    one, three, two = (shift(sent, dim, k).astype(f32) for k in (1, 3, 2))
    return lax.reduce_precision((v + two) + (one + three), 8, 7)


def shards(x, u, region, tally, lut, e_in, part, temp, triple, x_out):
    w, fg, xin, u_kept, keep, send, cw, pblk = first_sweep(
        x, u, region, tally, lut, e_in, x_out, part, temp
    )
    sums = keep + swap(send)
    sums = ring_sum(sums, 2)
    y = moment("xin_moment", tally, xin, w)
    sums, y = lax.optimization_barrier((sums, y))
    sums = ring_sum(sums, 1)
    z = moment("u_moment", tally, u_kept, w)
    sums, z = lax.optimization_barrier((sums, z))
    sums = ring_sum(sums, 0)
    mine = middle(sums, triple)
    theirs = swap(mine)
    w_qkv = (mine[192:224] + theirs[192:224])[:, 0:96]

    gs, pq, keep, send = second_sweep(
        tally, region, temp, xin, w, fg, mine, theirs, e_in, pblk, part, cw, y, z
    )
    own, p1, p2, p3 = pieces(keep, swap(send))
    r1, r2, r3 = shift(p1, 2, 1), shift(p2, 2, 2), shift(p3, 2, 3)
    grad_points = points(tally, gs, w, pq, 0, STEPS // 2)
    total = (own + r1.astype(f32)) + (r2.astype(f32) + r3.astype(f32))
    total = lax.reduce_precision(total, 8, 7)
    total, grad_points = lax.optimization_barrier((total, grad_points))
    total = ring_sum_b(total, 1)
    grad_points = points(tally, gs, w, pq, STEPS // 2, STEPS // 2, grad_points)
    total, grad_points = lax.optimization_barrier((total, grad_points))
    total = ring_sum_b(total, 0)
    mine = total.astype(bf16)
    mine = jnp.stack([mine] + [shift(mine, 2, k) for k in (1, 2, 3)])
    patch, w_in, w_slice, w_temp, w_out = final(mine, swap(mine))
    return grad_points, patch, w_in, w_slice, w_temp.reshape(H), w_qkv, w_out


def solution(mesh):
    rows = P(("pts", "grp"), None)
    return jax.shard_map(
        shards,
        mesh=mesh,
        in_specs=(rows, rows) + (P(),) * 8,
        out_specs=(rows,) + (P(),) * 6,
        check_vma=False,
    )
```

time: 999 us -> 114 us (0.11); the launches traced: 987 us -> 113 us
  matrix products: 348 us -> 0 us
  waiting for transfers between devices: 156 us -> 21.2 us
  blocking collectives: 133 us -> 0 us
  other arithmetic: 126 us -> 0.9 us
  local copies, waits for them, and re-layouts: 122 us -> 3.37 us
  loops' own time: 87.7 us -> 0 us
  starting transfers between devices: 0.08 us -> 48.2 us
  Pallas kernels: 0 us -> 38.3 us
  between operations: 14.2 us -> 0.86 us
    dot_general x249 -> x0, matrix products: 329 us -> none  [the longest x32 38.9 us: grad_y_of(): lax.dot_general(cotangent_row_values, exit_matrix, (((1,), (1,)), ((), ()...]
    psum x2 -> x0, waiting for transfers between devices: 156 us -> none  [the longest x1 80 us: shards(): lax.psum((parameter_derivatives[0], parameter_derivatives[1], parameter_d...]
    psum x2 -> x0, blocking collectives: 133 us -> none  [the longest x1 69 us: shards(): norm, raw, grad_otb = lax.psum((sums[0], sums[1], sums[2]), ('pts', 'grp'))]
    another operation x2 -> x0, loops' own time: 87.7 us -> none  [the longest x1 44 us: shards(): lax.fori_loop(first, own_count, first_kept, start_state)]
    add x81 -> x5, other arithmetic: 72.7 us -> 0.67 us  [the longest x1 0.61 us: shards(): w_qkv = (mine[192:224] + theirs[192:224])[:, 0:96]]
    dynamic_slice x50 -> x0, local copies, waits for them, and re-layouts: 51.3 us -> none  [the longest x32 29 us: locate(): return (row_start, x_rows, cotangent_row_values, patch_ids[patch_slot])]
    ppermute x0 -> x25, starting transfers between devices: none -> 48.2 us  [the longest x21 39 us: shift(): return lax.ppermute(v, 'pts', shift_pairs(dim, k))]
    pallas_call x0 -> x9, Pallas kernels: none -> 38.3 us  [the longest x1 10.3 us: first_sweep(): pl.pallas_call(first_kernel, in_specs=[in_smem(), in_vmem(), in_smem()] +...]
  transfers between devices with their start and end apart: 2 -> 25, of which waited for: 2 -> 15; matrix products, arithmetic and copies ran while one was open for 0% -> 1% of each run, Pallas kernels for 0% -> 12%
where the time goes in v1:
time: 114 us; the launch traced here: 113 us
  starting transfers between devices  48.2 us (42%)
  Pallas kernels  38.3 us (34%)
  waiting for transfers between devices  21.2 us (19%)
  local copies, waits for them, and re-layouts  3.37 us (3%)
    ppermute x21, starting transfers between devices, shift(): return lax.ppermute(v, 'pts', shift_pairs(dim, k))  39 us
    ppermute x21, waiting for transfers between devices, shift(): return lax.ppermute(v, 'pts', shift_pairs(dim, k))  16.6 us
    pallas_call x1, Pallas kernels, first_sweep(): pl.pallas_call(first_kernel, in_specs=[in_smem(), in_vmem(), in_smem()] +...  10.3 us
    pallas_call x1, Pallas kernels, second_sweep(): pl.pallas_call(second_kernel, in_specs=[in_smem(), in_vmem(), in_smem()]...  9.93 us
    ppermute x4, starting transfers between devices, swap(): return lax.ppermute(v, 'grp', [(0, 1), (1, 0)])  9.2 us
    pallas_call x2, Pallas kernels, points(): pl.pallas_call(functools.partial(points_kernel, first, number), in_specs=...  7.56 us
    pallas_call x2, Pallas kernels, moment(): pl.pallas_call(moment_kernel, in_specs=[in_smem(), in_vmem(), in_vmem()],...  5.71 us
    ppermute x4, waiting for transfers between devices, swap(): return lax.ppermute(v, 'grp', [(0, 1), (1, 0)])  4.57 us
  transfers between devices with their start and end apart: 25, of which 15 were waited for; matrix products, arithmetic and copies ran while one was open for 1% of the time, Pallas kernels for 12%

profile of v1, /device:TPU:1, one launch (start us, length us, event | category | flops | bytes accessed | tf_op | source)
XLA Modules:
  0.0 112.8 jit_solution(8103069216018161679)
XLA Ops:
  0.6 0.8 copy.22.tally_ref
  1.4 0.8 copy.23.region_ref
  2.2 0.6 copy-done.6
  2.9 10.3 %first_sweep.1 = (bf16[8,512,1024]{2,1,0:T(8,128)(2,1)S(1)}, bf16[8,512,1024]{2,1,0:T(8,128)(2,1)S(1)}, bf16[8,1024,256]{2,1,0:T(8,128)(2,1)S(1)}, bf16[8,1024,2...) custom-call(s32[64,2]{1,0:T(8,128)S(1)} %copy.22.tally_ref, ...), custom_call_target="tpu_custom_call" | custom-call | tf_op jit(solution)/shard_map/first_sweep/pallas_call | solution.py:245
  13.2 0.1 collective-permute-start
  13.3 1.2 %collective-permute-done = f32[136,128]{1,0:T(8,128)S(1)} collective-permute-done((f32[136,128]{1,0:T(8,128)S(1)}, f32[136,128]{1,0:T(8,128)S(1)}, u32[]{:S(2)}, u32[]{:S(2)}) %collective-permute-start) | collective-permute-done | bytes 69664 | tf_op jit(solution)/shard_map/ppermute | solution.py:623
  14.5 1.1 %collective-permute-start.2 = (f32[136,128]{1,0:T(8,128)S(1)}, f32[136,128]{1,0:T(8,128)S(1)}, u32[]{:S(2)}, u32[]{:S(2)}) collective-permute-start(f32[136,128]{1,0:T(8,128)S(1)} %add.60), channel_id=1, source_target_pairs={{0,2},{2,4},{4,6},{6,0},{8,10},{10,12},{12,14},{14,8},{16,18},{18,... | collective-permute-start | bytes 208904 | tf_op jit(solution)/shard_map/ppermute | solution.py:619
  15.7 3.6 %collective-permute-start.3 = (f32[136,128]{1,0:T(8,128)S(1)}, f32[136,128]{1,0:T(8,128)S(1)}, u32[]{:S(2)}, u32[]{:S(2)}) collective-permute-start(f32[136,128]{1,0:T(8,128)S(1)} %add.60), channel_id=1, source_target_pairs={{0,6},{2,0},{4,2},{6,4},{8,14},{10,8},{12,10},{14,12},{16,22},{18,... | collective-permute-start | bytes 208904 | tf_op jit(solution)/shard_map/ppermute | solution.py:619
  19.3 1.1 collective-permute-start.1
  20.4 2.9 %xin_moment.1.y_ref = f32[512,256]{1,0:T(8,128)S(1)} custom-call(s32[64,2]{1,0:T(8,128)S(1)} %copy.22.tally_ref, bf16[8,1024,256]{2,1,0:T(8,128)(2,1)S(1)} %get-tuple-element.36.rows_ref.xin_ref, bf16[8,512,1024]{2,1,0:T(8,128)(2,1)S(1)} %get-tuple-element.37.w_ref), custom_call_target="tpu_custom_call" | custom-call | flops 2147483648 | bytes 8388608 | tf_op jit(solution)/shard_map/xin_moment/pallas_call | solution.py:286
  23.2 0.0 copy-start
  23.2 0.0 collective-permute-done.2
  23.2 0.0 collective-permute-done.3
  23.3 0.7 collective-permute-done.1
  23.9 0.5 collective-permute-start.5
  24.5 2.2 %collective-permute-start.6 = (f32[136,128]{1,0:T(8,128)S(1)}, f32[136,128]{1,0:T(8,128)S(1)}, u32[]{:S(2)}, u32[]{:S(2)}) collective-permute-start(f32[136,128]{1,0:T(8,128)S(1)} %add_add_fusion.2), channel_id=1, source_target_pairs={{0,24},{2,26},{4,28},{6,30},{8,0},{10,2},{12,4},{14,6},{16,8},{18,... | collective-permute-start | bytes 208904 | tf_op jit(solution)/shard_map/ppermute | solution.py:619
  26.7 0.6 collective-permute-start.4
  27.2 2.9 %u_moment.1.z_ref = f32[512,256]{1,0:T(8,128)S(1)} custom-call(s32[64,2]{1,0:T(8,128)S(1)} %copy.22.tally_ref, bf16[8,1024,256]{2,1,0:T(8,128)(2,1)S(1)} %get-tuple-element.42.rows_ref, bf16[8,512,1024]{2,1,0:T(8,128)(2,1)S(1)} %get-tuple-element.37.w_ref), custom_call_target="tpu_custom_call" | custom-call | flops 2147483648 | bytes 8388608 | tf_op jit(solution)/shard_map/u_moment/pallas_call | solution.py:286
  30.1 0.0 copy-start.1
  30.1 0.0 collective-permute-done.5
  30.1 0.0 collective-permute-done.6
  30.2 1.4 %collective-permute-done.4 = f32[136,128]{1,0:T(8,128)S(1)} collective-permute-done((f32[136,128]{1,0:T(8,128)S(1)}, f32[136,128]{1,0:T(8,128)S(1)}, u32[]{:S(2)}, u32[]{:S(2)}) %collective-permute-start.4) | collective-permute-done | bytes 69664 | tf_op jit(solution)/shard_map/ppermute | solution.py:619
  31.6 1.4 %collective-permute-start.8 = (f32[136,128]{1,0:T(8,128)S(1)}, f32[136,128]{1,0:T(8,128)S(1)}, u32[]{:S(2)}, u32[]{:S(2)}) collective-permute-start(f32[136,128]{1,0:T(8,128)S(1)} %add_add_fusion.1), channel_id=1, source_target_pairs={{0,32},{2,34},{4,36},{6,38},{8,40},{10,42},{12,44},{14,46},{16,48}... | collective-permute-start | bytes 208904 | tf_op jit(solution)/shard_map/ppermute | solution.py:619
  33.0 9.5 %collective-permute-start.9 = (f32[136,128]{1,0:T(8,128)S(1)}, f32[136,128]{1,0:T(8,128)S(1)}, u32[]{:S(2)}, u32[]{:S(2)}) collective-permute-start(f32[136,128]{1,0:T(8,128)S(1)} %add_add_fusion.1), channel_id=1, source_target_pairs={{0,96},{2,98},{4,100},{6,102},{8,104},{10,106},{12,108},{14,110},{... | collective-permute-start | bytes 208904 | tf_op jit(solution)/shard_map/ppermute | solution.py:619
  42.5 2.3 %collective-permute-start.7 = (f32[136,128]{1,0:T(8,128)S(1)}, f32[136,128]{1,0:T(8,128)S(1)}, u32[]{:S(2)}, u32[]{:S(2)}) collective-permute-start(f32[136,128]{1,0:T(8,128)S(1)} %add_add_fusion.1), channel_id=1, source_target_pairs={{0,64},{2,66},{4,68},{6,70},{8,72},{10,74},{12,76},{14,78},{16,80}... | collective-permute-start | bytes 208904 | tf_op jit(solution)/shard_map/ppermute | solution.py:619
  44.8 2.5 %collective-permute-done.7 = f32[136,128]{1,0:T(8,128)S(1)} collective-permute-done((f32[136,128]{1,0:T(8,128)S(1)}, f32[136,128]{1,0:T(8,128)S(1)}, u32[]{:S(2)}, u32[]{:S(2)}) %collective-permute-start.7) | collective-permute-done | bytes 69664 | tf_op jit(solution)/shard_map/ppermute | solution.py:619
  47.3 3.6 %middle.1.mine_ref = f32[224,128]{1,0:T(8,128)S(1)} custom-call(f32[136,128]{1,0:T(8,128)S(1)} %add_add_fusion.s_ref, bf16[32,96]{1,0:T(8,128)(2,1)S(1)} %copy-done.5), custom_call_target="tpu_custom_call" | custom-call | tf_op jit(solution)/shard_map/middle/pallas_call | solution.py:354
  50.9 4.2 %collective-permute-start.10 = (f32[224,128]{1,0:T(8,128)S(1)}, f32[224,128]{1,0:T(8,128)S(1)}, u32[]{:S(2)}, u32[]{:S(2)}) collective-permute-start(f32[224,128]{1,0:T(8,128)S(1)} %middle.1.mine_ref), channel_id=1, source_target_pairs={{0,1},{1,0},{2,3},{3,2},{4,5},{5,4},{6,7},{7,6},{8,9},{9,8},{10,11... | collective-permute-start | bytes 344072 | tf_op jit(solution)/shard_map/ppermute | solution.py:623
  55.1 1.0 collective-permute-done.10.theirs_ref
  56.0 9.9 %second_sweep.1 = (bf16[8,512,1024]{2,1,0:T(8,128)(2,1)S(1)}, bf16[256,1024]{1,0:T(8,128)(2,1)S(1)}, f32[704,256]{1,0:T(8,128)}, bf16[704,256]{1,0:T(8,128)(2,1)S(1)}) custom-call(s32[64,2]{1,0:T(8,128)S(1)} %copy.22.tally_ref, s32[64,2,16]{2,1,0:T(2,128)S(1)} %copy.23.region_ref, f32[8]{0:T(128)S(1)} %copy-done.7, f32[1,8]{1,0:T(1,128)S(1)} %bitcast.6, ...), custom_call_target="tpu_custom_call" | custom-call | tf_op jit(solution)/shard_map/second_sweep/pallas_call | solution.py:477
  66.0 1.7 %collective-permute-done.11.recv_ref = bf16[704,256]{1,0:T(8,128)(2,1)S(1)} collective-permute-done((bf16[704,256]{1,0:T(8,128)(2,1)S(1)}, bf16[704,256]{1,0:T(8,128)(2,1)S(1)}, u32[]{:S(2)}, u32[]{:S(2)}) %collective-permute-start.11) | collective-permute-done | bytes 360480 | tf_op jit(solution)/shard_map/ppermute | solution.py:623
  67.6 1.1 copy-done.3
  68.8 0.1 pieces.1
  68.8 0.6 collective-permute-start.14
  69.5 0.9 collective-permute-start.12
  70.4 5.1 %points.2.refs_0_ = bf16[8192,256]{1,0:T(8,128)(2,1)} custom-call(s32[64,2]{1,0:T(8,128)S(1)} %copy.22.tally_ref, bf16[8,512,1024]{2,1,0:T(8,128)(2,1)S(1)} %get-tuple-element.54.gs_ref, bf16[8,512,1024]{2,1,0:T(8,128)(2,1)S(1)} %get-tuple-element.37.w_ref, bf16[256,1024]{1,0:T(8,128)(2,1)S(1)} %get-tuple-element.55.pq_ref), custom_call_target="tpu_custom_call" | custom-call | flops 2147483648 | bytes 4194304 | tf_op jit(solution)/shard_map/points/pallas_call | solution.py:534
  75.5 0.0 collective-permute-done.14
  75.5 0.0 collective-permute-done.13
  75.5 2.0 %collective-permute-done.12 = bf16[176,256]{1,0:T(8,128)(2,1)S(1)} collective-permute-done((bf16[176,256]{1,0:T(8,128)(2,1)S(1)}, bf16[176,256]{1,0:T(8,128)(2,1)S(1)}, u32[]{:S(2)}, u32[]{:S(2)}) %collective-permute-start.12) | collective-permute-done | bytes 90144 | tf_op jit(solution)/shard_map/ppermute | solution.py:619
  77.5 0.1 add_reduce-precision_fusion.1
  77.5 0.1 collective-permute-start.17
  77.6 1.5 %collective-permute-start.16 = (bf16[176,256]{1,0:T(8,128)(2,1)S(1)}, bf16[176,256]{1,0:T(8,128)(2,1)S(1)}, u32[]{:S(2)}, u32[]{:S(2)}) collective-permute-start(bf16[176,256]{1,0:T(8,128)(2,1)S(1)} %convert_element_type.39), channel_id=1, source_target_pairs={{0,8},{2,10},{4,12},{6,14},{8,16},{10,18},{12,20},{14,22},{16,24},... | collective-permute-start | bytes 270344 | tf_op jit(solution)/shard_map/ppermute | solution.py:619
  79.1 0.2 collective-permute-start.15
  79.3 2.5 %points.3 = bf16[8192,256]{1,0:T(8,128)(2,1)} custom-call(s32[64,2]{1,0:T(8,128)S(1)} %copy.22.tally_ref, bf16[8,512,1024]{2,1,0:T(8,128)(2,1)S(1)} %get-tuple-element.54.gs_ref, bf16[8,512,1024]{2,1,0:T(8,128)(2,1)S(1)} %get-tuple-element.37.w_ref, bf16[256,1024]{1,0:T(8,128)(2,1)S(1)} %get-tuple-element.55.pq_ref, ...), custom_call_target="tpu_custom_call", output_to_operand_aliasing={{}: (4, {})} | custom-call | flops 2147483648 | bytes 4194304 | tf_op jit(solution)/shard_map/points/pallas_call | solution.py:534
  81.8 0.5 collective-permute-done.16
  82.3 1.8 %collective-permute-done.15 = bf16[176,256]{1,0:T(8,128)(2,1)S(1)} collective-permute-done((bf16[176,256]{1,0:T(8,128)(2,1)S(1)}, bf16[176,256]{1,0:T(8,128)(2,1)S(1)}, u32[]{:S(2)}, u32[]{:S(2)}) %collective-permute-start.15) | collective-permute-done | bytes 90144 | tf_op jit(solution)/shard_map/ppermute | solution.py:619
  84.1 0.1 add_reduce-precision_fusion
  84.1 6.4 %collective-permute-start.20 = (bf16[176,256]{1,0:T(8,128)(2,1)S(1)}, bf16[176,256]{1,0:T(8,128)(2,1)S(1)}, u32[]{:S(2)}, u32[]{:S(2)}) collective-permute-start(bf16[176,256]{1,0:T(8,128)(2,1)S(1)} %convert_element_type.43), channel_id=1, source_target_pairs={{0,96},{2,98},{4,100},{6,102},{8,104},{10,106},{12,108},{14,110},{... | collective-permute-start | bytes 270344 | tf_op jit(solution)/shard_map/ppermute | solution.py:619
  90.5 0.0 collective-permute-start.19
  90.5 3.7 %collective-permute-start.18 = (bf16[176,256]{1,0:T(8,128)(2,1)S(1)}, bf16[176,256]{1,0:T(8,128)(2,1)S(1)}, u32[]{:S(2)}, u32[]{:S(2)}) collective-permute-start(bf16[176,256]{1,0:T(8,128)(2,1)S(1)} %convert_element_type.43), channel_id=1, source_target_pairs={{0,64},{2,66},{4,68},{6,70},{8,72},{10,74},{12,76},{14,78},{16,80}... | collective-permute-start | bytes 270344 | tf_op jit(solution)/shard_map/ppermute | solution.py:619
  94.2 0.0 collective-permute-done.20
  94.2 0.9 collective-permute-done.19
  95.1 2.0 %collective-permute-done.18 = bf16[176,256]{1,0:T(8,128)(2,1)S(1)} collective-permute-done((bf16[176,256]{1,0:T(8,128)(2,1)S(1)}, bf16[176,256]{1,0:T(8,128)(2,1)S(1)}, u32[]{:S(2)}, u32[]{:S(2)}) %collective-permute-start.18) | collective-permute-done | bytes 90144 | tf_op jit(solution)/shard_map/ppermute | solution.py:619
  97.1 0.1 reduce-precision_convert_fusion
  97.1 2.7 %collective-permute-start.23 = (bf16[176,256]{1,0:T(8,128)(2,1)S(1)}, bf16[176,256]{1,0:T(8,128)(2,1)S(1)}, u32[]{:S(2)}, u32[]{:S(2)}) collective-permute-start(bf16[176,256]{1,0:T(8,128)(2,1)S(1)} %reduce-precision_convert_fusion), channel_id=1, source_target_pairs={{0,6},{2,0},{4,2},{6,4},{8,14},{10,8},{12,10},{14,12},{16,22},{18,... | collective-permute-start | bytes 270344 | tf_op jit(solution)/shard_map/ppermute | solution.py:619
  99.8 0.0 collective-permute-start.22
  99.8 0.7 collective-permute-start.21
  100.5 1.8 %collective-permute-done.23 = bf16[176,256]{1,0:T(8,128)(2,1)S(1)} collective-permute-done((bf16[176,256]{1,0:T(8,128)(2,1)S(1)}, bf16[176,256]{1,0:T(8,128)(2,1)S(1)}, u32[]{:S(2)}, u32[]{:S(2)}) %collective-permute-start.23) | collective-permute-done | bytes 90144 | tf_op jit(solution)/shard_map/ppermute | solution.py:619
  102.2 2.5 %collective-permute-done.22 = bf16[176,256]{1,0:T(8,128)(2,1)S(1)} collective-permute-done((bf16[176,256]{1,0:T(8,128)(2,1)S(1)}, bf16[176,256]{1,0:T(8,128)(2,1)S(1)}, u32[]{:S(2)}, u32[]{:S(2)}) %collective-permute-start.22) | collective-permute-done | bytes 90144 | tf_op jit(solution)/shard_map/ppermute | solution.py:619
  104.8 0.6 collective-permute-done.21
  105.4 4.9 %collective-permute-start.24 = (bf16[4,176,256]{2,1,0:T(8,128)(2,1)S(1)}, bf16[4,176,256]{2,1,0:T(8,128)(2,1)S(1)}, u32[]{:S(2)}, u32[]{:S(2)}) collective-permute-start(bf16[4,176,256]{2,1,0:T(8,128)(2,1)S(1)} %pad_maximum_fusion.mine_ref), channel_id=1, source_target_pairs={{0,1},{1,0},{2,3},{3,2},{4,5},{5,4},{6,7},{7,6},{8,9},{9,8},{10,11... | collective-permute-start | bytes 1081352 | tf_op jit(solution)/shard_map/ppermute | solution.py:623
  110.3 0.6 slice_add_fusion
  110.9 0.7 collective-permute-done.24.theirs_ref
  111.6 1.2 %final.1 = (f32[512,256]{1,0:T(8,128)}, f32[256,512]{1,0:T(8,128)}, f32[32,64]{1,0:T(8,128)}, f32[1,8]{1,0:T(1,128)}, f32[256,256]{1,0:T(8,128)}) custom-call(bf16[4,176,256]{2,1,0:T(8,128)(2,1)S(1)} %pad_maximum_fusion.mine_ref, bf16[4,176,256]{2,1,0:T(8,128)(2,1)S(1)} %collective-permute-done.24.theirs_ref), custom_call_target="tpu_custom_call" | custom-call | tf_op jit(solution)/shard_map/final/pallas_call | solution.py:592
  (26 shorter events, 0.2 us)
Async XLA Ops:
  2.2 0.7 copy-start.6
  13.2 1.3 %collective-permute-start = (f32[136,128]{1,0:T(8,128)S(1)}, f32[136,128]{1,0:T(8,128)S(1)}, u32[]{:S(2)}, u32[]{:S(2)}) collective-permute-start(f32[136,128]{1,0:T(8,128)S(1)} %get-tuple-element.40), channel_id=1, source_target_pairs={{0,1},{1,0},{2,3},{3,2},{4,5},{5,4},{6,7},{7,6},{8,9},{9,8},{10,11... | collective-permute-start | bytes 208904 | tf_op jit(solution)/shard_map/ppermute | solution.py:623
  14.5 8.7 %collective-permute-start.2 = (f32[136,128]{1,0:T(8,128)S(1)}, f32[136,128]{1,0:T(8,128)S(1)}, u32[]{:S(2)}, u32[]{:S(2)}) collective-permute-start(f32[136,128]{1,0:T(8,128)S(1)} %add.60), channel_id=1, source_target_pairs={{0,2},{2,4},{4,6},{6,0},{8,10},{10,12},{12,14},{14,8},{16,18},{18,... | collective-permute-start | bytes 208904 | tf_op jit(solution)/shard_map/ppermute | solution.py:619
  15.7 7.6 %collective-permute-start.3 = (f32[136,128]{1,0:T(8,128)S(1)}, f32[136,128]{1,0:T(8,128)S(1)}, u32[]{:S(2)}, u32[]{:S(2)}) collective-permute-start(f32[136,128]{1,0:T(8,128)S(1)} %add.60), channel_id=1, source_target_pairs={{0,6},{2,0},{4,2},{6,4},{8,14},{10,8},{12,10},{14,12},{16,22},{18,... | collective-permute-start | bytes 208904 | tf_op jit(solution)/shard_map/ppermute | solution.py:619
  19.3 4.7 %collective-permute-start.1 = (f32[136,128]{1,0:T(8,128)S(1)}, f32[136,128]{1,0:T(8,128)S(1)}, u32[]{:S(2)}, u32[]{:S(2)}) collective-permute-start(f32[136,128]{1,0:T(8,128)S(1)} %add.60), channel_id=1, source_target_pairs={{0,4},{2,6},{4,0},{6,2},{8,12},{10,14},{12,8},{14,10},{16,20},{18,... | collective-permute-start | bytes 208904 | tf_op jit(solution)/shard_map/ppermute | solution.py:619
  23.2 6.9 %copy-start = (f32[512,256]{1,0:T(8,128)}, f32[512,256]{1,0:T(8,128)S(1)}, u32[]{:S(2)}) copy-start(f32[512,256]{1,0:T(8,128)S(1)} %xin_moment.1.y_ref) | copy-start | bytes 1572868
  23.9 6.2 %collective-permute-start.5 = (f32[136,128]{1,0:T(8,128)S(1)}, f32[136,128]{1,0:T(8,128)S(1)}, u32[]{:S(2)}, u32[]{:S(2)}) collective-permute-start(f32[136,128]{1,0:T(8,128)S(1)} %add_add_fusion.2), channel_id=1, source_target_pairs={{0,8},{2,10},{4,12},{6,14},{8,16},{10,18},{12,20},{14,22},{16,24},... | collective-permute-start | bytes 208904 | tf_op jit(solution)/shard_map/ppermute | solution.py:619
  24.5 5.7 %collective-permute-start.6 = (f32[136,128]{1,0:T(8,128)S(1)}, f32[136,128]{1,0:T(8,128)S(1)}, u32[]{:S(2)}, u32[]{:S(2)}) collective-permute-start(f32[136,128]{1,0:T(8,128)S(1)} %add_add_fusion.2), channel_id=1, source_target_pairs={{0,24},{2,26},{4,28},{6,30},{8,0},{10,2},{12,4},{14,6},{16,8},{18,... | collective-permute-start | bytes 208904 | tf_op jit(solution)/shard_map/ppermute | solution.py:619
  26.7 4.9 %collective-permute-start.4 = (f32[136,128]{1,0:T(8,128)S(1)}, f32[136,128]{1,0:T(8,128)S(1)}, u32[]{:S(2)}, u32[]{:S(2)}) collective-permute-start(f32[136,128]{1,0:T(8,128)S(1)} %add_add_fusion.2), channel_id=1, source_target_pairs={{0,16},{2,18},{4,20},{6,22},{8,24},{10,26},{12,28},{14,30},{16,0},... | collective-permute-start | bytes 208904 | tf_op jit(solution)/shard_map/ppermute | solution.py:619
  27.2 20.0 %copy-start.5 = (bf16[32,96]{1,0:T(8,128)(2,1)S(1)}, bf16[32,96]{1,0:T(8,128)(2,1)}, u32[]{:S(2)}) copy-start(bf16[32,96]{1,0:T(8,128)(2,1)} %t_ref.1) | copy-start | bytes 18436
  27.2 28.8 %copy-start.2 = (bf16[256,512]{1,0:T(8,128)(2,1)S(1)}, bf16[256,512]{1,0:T(8,128)(2,1)}, u32[]{:S(2)}) copy-start(bf16[256,512]{1,0:T(8,128)(2,1)} %e_in_ref.1) | copy-start | bytes 786436
  27.2 28.8 %copy-start.4 = (bf16[32,64]{1,0:T(8,128)(2,1)S(1)}, bf16[32,64]{1,0:T(8,128)(2,1)}, u32[]{:S(2)}) copy-start(bf16[32,64]{1,0:T(8,128)(2,1)} %p_ref.1) | copy-start | bytes 12292
  27.2 28.8 %copy-start.7 = (f32[8]{0:T(128)S(1)}, f32[8]{0:T(128)}, u32[]{:S(2)}) copy-start(f32[8]{0:T(128)} %temp_ref.3) | copy-start | bytes 100
  30.1 25.9 %copy-start.1 = (f32[512,256]{1,0:T(8,128)}, f32[512,256]{1,0:T(8,128)S(1)}, u32[]{:S(2)}) copy-start(f32[512,256]{1,0:T(8,128)S(1)} %u_moment.1.z_ref) | copy-start | bytes 1572868
  31.6 13.2 %collective-permute-start.8 = (f32[136,128]{1,0:T(8,128)S(1)}, f32[136,128]{1,0:T(8,128)S(1)}, u32[]{:S(2)}, u32[]{:S(2)}) collective-permute-start(f32[136,128]{1,0:T(8,128)S(1)} %add_add_fusion.1), channel_id=1, source_target_pairs={{0,32},{2,34},{4,36},{6,38},{8,40},{10,42},{12,44},{14,46},{16,48}... | collective-permute-start | bytes 208904 | tf_op jit(solution)/shard_map/ppermute | solution.py:619
  33.0 11.8 %collective-permute-start.9 = (f32[136,128]{1,0:T(8,128)S(1)}, f32[136,128]{1,0:T(8,128)S(1)}, u32[]{:S(2)}, u32[]{:S(2)}) collective-permute-start(f32[136,128]{1,0:T(8,128)S(1)} %add_add_fusion.1), channel_id=1, source_target_pairs={{0,96},{2,98},{4,100},{6,102},{8,104},{10,106},{12,108},{14,110},{... | collective-permute-start | bytes 208904 | tf_op jit(solution)/shard_map/ppermute | solution.py:619
  42.5 4.8 %collective-permute-start.7 = (f32[136,128]{1,0:T(8,128)S(1)}, f32[136,128]{1,0:T(8,128)S(1)}, u32[]{:S(2)}, u32[]{:S(2)}) collective-permute-start(f32[136,128]{1,0:T(8,128)S(1)} %add_add_fusion.1), channel_id=1, source_target_pairs={{0,64},{2,66},{4,68},{6,70},{8,72},{10,74},{12,76},{14,78},{16,80}... | collective-permute-start | bytes 208904 | tf_op jit(solution)/shard_map/ppermute | solution.py:619
  50.9 5.2 %collective-permute-start.10 = (f32[224,128]{1,0:T(8,128)S(1)}, f32[224,128]{1,0:T(8,128)S(1)}, u32[]{:S(2)}, u32[]{:S(2)}) collective-permute-start(f32[224,128]{1,0:T(8,128)S(1)} %middle.1.mine_ref), channel_id=1, source_target_pairs={{0,1},{1,0},{2,3},{3,2},{4,5},{5,4},{6,7},{7,6},{8,9},{9,8},{10,11... | collective-permute-start | bytes 344072 | tf_op jit(solution)/shard_map/ppermute | solution.py:623
  66.0 1.7 %collective-permute-start.11 = (bf16[704,256]{1,0:T(8,128)(2,1)S(1)}, bf16[704,256]{1,0:T(8,128)(2,1)S(1)}, u32[]{:S(2)}, u32[]{:S(2)}) collective-permute-start(bf16[704,256]{1,0:T(8,128)(2,1)S(1)} %get-tuple-element.49), channel_id=1, source_target_pairs={{0,1},{1,0},{2,3},{3,2},{4,5},{5,4},{6,7},{7,6},{8,9},{9,8},{10,11... | collective-permute-start | bytes 1081352 | tf_op jit(solution)/shard_map/ppermute | solution.py:623
  67.6 1.1 copy-start.3
  68.8 6.6 %collective-permute-start.14 = (bf16[176,256]{1,0:T(8,128)(2,1)S(1)}, bf16[176,256]{1,0:T(8,128)(2,1)S(1)}, u32[]{:S(2)}, u32[]{:S(2)}) collective-permute-start(bf16[176,256]{1,0:T(8,128)(2,1)S(1)} %get-tuple-element.53), channel_id=1, source_target_pairs={{0,6},{2,0},{4,2},{6,4},{8,14},{10,8},{12,10},{14,12},{16,22},{18,... | collective-permute-start | bytes 270344 | tf_op jit(solution)/shard_map/ppermute | solution.py:619
  69.5 6.0 %collective-permute-start.13 = (bf16[176,256]{1,0:T(8,128)(2,1)S(1)}, bf16[176,256]{1,0:T(8,128)(2,1)S(1)}, u32[]{:S(2)}, u32[]{:S(2)}) collective-permute-start(bf16[176,256]{1,0:T(8,128)(2,1)S(1)} %get-tuple-element.52), channel_id=1, source_target_pairs={{0,4},{2,6},{4,0},{6,2},{8,12},{10,14},{12,8},{14,10},{16,20},{18,... | collective-permute-start | bytes 270344 | tf_op jit(solution)/shard_map/ppermute | solution.py:619
  69.5 8.0 %collective-permute-start.12 = (bf16[176,256]{1,0:T(8,128)(2,1)S(1)}, bf16[176,256]{1,0:T(8,128)(2,1)S(1)}, u32[]{:S(2)}, u32[]{:S(2)}) collective-permute-start(bf16[176,256]{1,0:T(8,128)(2,1)S(1)} %get-tuple-element.51), channel_id=1, source_target_pairs={{0,2},{2,4},{4,6},{6,0},{8,10},{10,12},{12,14},{14,8},{16,18},{18,... | collective-permute-start | bytes 270344 | tf_op jit(solution)/shard_map/ppermute | solution.py:619
  77.5 4.2 %collective-permute-start.17 = (bf16[176,256]{1,0:T(8,128)(2,1)S(1)}, bf16[176,256]{1,0:T(8,128)(2,1)S(1)}, u32[]{:S(2)}, u32[]{:S(2)}) collective-permute-start(bf16[176,256]{1,0:T(8,128)(2,1)S(1)} %convert_element_type.39), channel_id=1, source_target_pairs={{0,24},{2,26},{4,28},{6,30},{8,0},{10,2},{12,4},{14,6},{16,8},{18,... | collective-permute-start | bytes 270344 | tf_op jit(solution)/shard_map/ppermute | solution.py:619
  77.6 4.7 %collective-permute-start.16 = (bf16[176,256]{1,0:T(8,128)(2,1)S(1)}, bf16[176,256]{1,0:T(8,128)(2,1)S(1)}, u32[]{:S(2)}, u32[]{:S(2)}) collective-permute-start(bf16[176,256]{1,0:T(8,128)(2,1)S(1)} %convert_element_type.39), channel_id=1, source_target_pairs={{0,8},{2,10},{4,12},{6,14},{8,16},{10,18},{12,20},{14,22},{16,24},... | collective-permute-start | bytes 270344 | tf_op jit(solution)/shard_map/ppermute | solution.py:619
  79.1 5.0 %collective-permute-start.15 = (bf16[176,256]{1,0:T(8,128)(2,1)S(1)}, bf16[176,256]{1,0:T(8,128)(2,1)S(1)}, u32[]{:S(2)}, u32[]{:S(2)}) collective-permute-start(bf16[176,256]{1,0:T(8,128)(2,1)S(1)} %convert_element_type.39), channel_id=1, source_target_pairs={{0,16},{2,18},{4,20},{6,22},{8,24},{10,26},{12,28},{14,30},{16,0},... | collective-permute-start | bytes 270344 | tf_op jit(solution)/shard_map/ppermute | solution.py:619
  84.1 10.1 %collective-permute-start.20 = (bf16[176,256]{1,0:T(8,128)(2,1)S(1)}, bf16[176,256]{1,0:T(8,128)(2,1)S(1)}, u32[]{:S(2)}, u32[]{:S(2)}) collective-permute-start(bf16[176,256]{1,0:T(8,128)(2,1)S(1)} %convert_element_type.43), channel_id=1, source_target_pairs={{0,96},{2,98},{4,100},{6,102},{8,104},{10,106},{12,108},{14,110},{... | collective-permute-start | bytes 270344 | tf_op jit(solution)/shard_map/ppermute | solution.py:619
  90.5 4.6 %collective-permute-start.19 = (bf16[176,256]{1,0:T(8,128)(2,1)S(1)}, bf16[176,256]{1,0:T(8,128)(2,1)S(1)}, u32[]{:S(2)}, u32[]{:S(2)}) collective-permute-start(bf16[176,256]{1,0:T(8,128)(2,1)S(1)} %convert_element_type.43), channel_id=1, source_target_pairs={{0,32},{2,34},{4,36},{6,38},{8,40},{10,42},{12,44},{14,46},{16,48}... | collective-permute-start | bytes 270344 | tf_op jit(solution)/shard_map/ppermute | solution.py:619
  90.5 6.6 %collective-permute-start.18 = (bf16[176,256]{1,0:T(8,128)(2,1)S(1)}, bf16[176,256]{1,0:T(8,128)(2,1)S(1)}, u32[]{:S(2)}, u32[]{:S(2)}) collective-permute-start(bf16[176,256]{1,0:T(8,128)(2,1)S(1)} %convert_element_type.43), channel_id=1, source_target_pairs={{0,64},{2,66},{4,68},{6,70},{8,72},{10,74},{12,76},{14,78},{16,80}... | collective-permute-start | bytes 270344 | tf_op jit(solution)/shard_map/ppermute | solution.py:619
  97.1 5.1 %collective-permute-start.23 = (bf16[176,256]{1,0:T(8,128)(2,1)S(1)}, bf16[176,256]{1,0:T(8,128)(2,1)S(1)}, u32[]{:S(2)}, u32[]{:S(2)}) collective-permute-start(bf16[176,256]{1,0:T(8,128)(2,1)S(1)} %reduce-precision_convert_fusion), channel_id=1, source_target_pairs={{0,6},{2,0},{4,2},{6,4},{8,14},{10,8},{12,10},{14,12},{16,22},{18,... | collective-permute-start | bytes 270344 | tf_op jit(solution)/shard_map/ppermute | solution.py:619
  99.8 5.0 %collective-permute-start.22 = (bf16[176,256]{1,0:T(8,128)(2,1)S(1)}, bf16[176,256]{1,0:T(8,128)(2,1)S(1)}, u32[]{:S(2)}, u32[]{:S(2)}) collective-permute-start(bf16[176,256]{1,0:T(8,128)(2,1)S(1)} %reduce-precision_convert_fusion), channel_id=1, source_target_pairs={{0,4},{2,6},{4,0},{6,2},{8,12},{10,14},{12,8},{14,10},{16,20},{18,... | collective-permute-start | bytes 270344 | tf_op jit(solution)/shard_map/ppermute | solution.py:619
  99.8 5.6 %collective-permute-start.21 = (bf16[176,256]{1,0:T(8,128)(2,1)S(1)}, bf16[176,256]{1,0:T(8,128)(2,1)S(1)}, u32[]{:S(2)}, u32[]{:S(2)}) collective-permute-start(bf16[176,256]{1,0:T(8,128)(2,1)S(1)} %reduce-precision_convert_fusion), channel_id=1, source_target_pairs={{0,2},{2,4},{4,6},{6,0},{8,10},{10,12},{12,14},{14,8},{16,18},{18,... | collective-permute-start | bytes 270344 | tf_op jit(solution)/shard_map/ppermute | solution.py:619
  105.4 6.2 %collective-permute-start.24 = (bf16[4,176,256]{2,1,0:T(8,128)(2,1)S(1)}, bf16[4,176,256]{2,1,0:T(8,128)(2,1)S(1)}, u32[]{:S(2)}, u32[]{:S(2)}) collective-permute-start(bf16[4,176,256]{2,1,0:T(8,128)(2,1)S(1)} %pad_maximum_fusion.mine_ref), channel_id=1, source_target_pairs={{0,1},{1,0},{2,3},{3,2},{4,5},{5,4},{6,7},{7,6},{8,9},{9,8},{10,11... | collective-permute-start | bytes 1081352 | tf_op jit(solution)/shard_map/ppermute | solution.py:623

commit v2 on v1

v2 whole, which is shorter than its diff:
```python
import functools
import math

import jax
import jax.numpy as jnp
from jax import lax
from jax.experimental import pallas as pl
from jax.experimental.pallas import tpu as pltpu
from jax.sharding import PartitionSpec as P

f32 = jnp.float32
bf16 = jnp.bfloat16
HIGH = lax.Precision.HIGHEST
EPS = 1e-05
LOG2E = math.log2(math.e)

ROWS = 512
BLOCKS = 16
STEP = 1024
STEPS = BLOCKS * ROWS // STEP
UNROLL = 4
C = 256
H = 8
D = 32
G = 64
HG = H * G
PATCHES = 512
SUMS = 136
MID = 224
PIECE = 176
HALF = 4 * PIECE
BUF = 2 * HALF
EXT = C + BLOCKS
LANES = 256
CHUNKS = STEP // LANES
UNITS = (16, 4, 1)
AXES = ((2, 1, 0), (1, 0, 2))
VMEM_LIMIT = 16 * 2**20
SMALL = pltpu.CompilerParams(vmem_limit_bytes=8 * 2**20)

NN = (((1,), (0,)), ((), ()))
NT = (((1,), (1,)), ((), ()))
TN = (((0,), (0,)), ((), ()))


def dot(a, b, dims, precision=None):
    return lax.dot_general(a, b, dims, precision=precision, preferred_element_type=f32)


def split(a):
    hi = a.astype(bf16)
    return hi, (a - hi.astype(f32)).astype(bf16)


def split3(a):
    hi, rest = a.astype(bf16), a - a.astype(bf16).astype(f32)
    return (hi, *split(rest))


def dot_left2(a, b, dims):
    hi, lo = split(a)
    return dot(hi, b, dims) + dot(lo, b, dims)


def dot_right2(a, b, dims):
    hi, lo = split(b)
    return dot(a, hi, dims) + dot(a, lo, dims)


def dot3(a, b, dims):
    (a_hi, a_lo), (b_hi, b_lo) = split(a), split(b)
    return dot(a_hi, b_hi, dims) + (dot(a_hi, b_lo, dims) + dot(a_lo, b_hi, dims))


def iota(shape, dim):
    return lax.broadcasted_iota(jnp.int32, shape, dim)


def head_mask(j, rows):
    return (iota((rows, 128), 1) >> 5) == j


def spread(packed):
    return jnp.concatenate([jnp.where(head_mask(j, G), packed, 0.0) for j in range(4)], axis=0)


def gather_heads(wide):
    total = jnp.where(head_mask(0, G), wide[0:G], 0.0)
    for j in range(1, 4):
        total = total + jnp.where(head_mask(j, G), wide[j * G : (j + 1) * G], 0.0)
    return total


def in_vmem():
    return pl.BlockSpec(memory_space=pltpu.VMEM)


def in_smem():
    return pl.BlockSpec(memory_space=pltpu.SMEM)


def in_hbm():
    return pl.BlockSpec(memory_space=pl.ANY)


def hbm(v):
    return pltpu.with_memory_space_constraint(v, pltpu.HBM)


def vmem(v):
    return pltpu.with_memory_space_constraint(v, pltpu.VMEM)


def place():
    return lax.axis_index("pts"), lax.axis_index("grp")


def ring_place(core):
    pts = lax.axis_index("pts")
    return jnp.where(core == 0, pts // UNITS[AXES[0][0]], pts // UNITS[AXES[1][0]]) & 3


def block_count(tally_ref):
    pts, grp = place()
    return tally_ref[grp, pts]


def step_count(tally_ref):
    return ((block_count(tally_ref) + 2 * UNROLL - 1) // (2 * UNROLL)) * UNROLL


def patch_onehot(region_ref):
    pts, grp = place()
    mine = iota((BLOCKS, 64), 1) == pts
    ids = jnp.sum(jnp.where(mine, region_ref[grp], 0), axis=1, keepdims=True)
    return (iota((BLOCKS, PATCHES), 1) == ids).astype(f32)


def first_kernel(
    tally_hbm,
    region_hbm,
    x_hbm,
    u_hbm,
    lut_hbm,
    e_in_hbm,
    x_out_hbm,
    p_hbm,
    temp_hbm,
    w_ref,
    fg_ref,
    xt_ref,
    u_ref,
    keep_ref,
    send_ref,
    pblk_ref,
    tally_ref,
    region_ref,
    temp_ref,
    x_ref,
    lut_ref,
    e_in_ref,
    x_out_ref,
    p_ref,
    et_ref,
    rows_ref,
    acc_ref,
    x_sem,
    u_sem,
    sem,
):
    small = [
        pltpu.make_async_copy(src, dst, sem.at[k])
        for k, (src, dst) in enumerate(
            (
                (e_in_hbm, e_in_ref),
                (p_hbm, p_ref),
                (lut_hbm, lut_ref),
                (x_out_hbm, x_out_ref),
                (temp_hbm, temp_ref),
                (tally_hbm, tally_ref),
                (region_hbm, region_ref),
            )
        )
    ]
    for copy in small:
        copy.start()

    def rows_copies(b):
        at = pl.ds(b * STEP if isinstance(b, int) else pl.multiple_of(b * STEP, STEP), STEP)
        return (
            pltpu.make_async_copy(x_hbm.at[at, :], x_ref.at[b], x_sem.at[b]),
            pltpu.make_async_copy(u_hbm.at[at, :], u_ref.at[b], u_sem.at[b]),
        )

    for b in range(STEPS):
        for copy in rows_copies(b):
            copy.start()

    acc_ref[...] = jnp.zeros_like(acc_ref)
    for b in range(STEPS):
        block = 2 * b + (iota((BLOCKS, STEP), 1) >> 9)
        xt_ref[b, C:EXT, :] = (iota((BLOCKS, STEP), 0) == block).astype(f32).astype(bf16)
        for q in range(2):
            fg_ref[b, q, C:EXT, :] = jnp.ones((BLOCKS, STEP), bf16)
    for copy in small:
        copy.wait()
    count = block_count(tally_ref)
    steps = step_count(tally_ref)
    onehot = patch_onehot(region_ref).astype(bf16)
    et_ref[...] = e_in_ref[...].T
    t1 = ((iota((HG, G), 0) & (G - 1)) == iota((HG, G), 1)).astype(f32).astype(bf16)
    t2 = (iota((D, C), 0) == (iota((D, C), 1) & (D - 1))).astype(f32).astype(bf16)
    tall = dot(t1, p_ref[...], NT).astype(bf16)
    tiled = dot(tall, t2, NN)
    own = (iota((HG, C), 0) >> 6) == (iota((HG, C), 1) >> 5)
    pblk_ref[...] = jnp.where(own, tiled, 0.0).astype(bf16)
    rows_ref[...] = dot(onehot, lut_ref[...], NN)

    def project(b, c):
        at = pl.ds(c * LANES, LANES)
        block = 2 * b + c * LANES // ROWS
        xin = x_ref[b, at, :] + rows_ref[pl.ds(block, 1), :].astype(bf16)
        xt_ref[b, 0:C, at] = xin.T
        proj = dot(et_ref[...], xin, NT).astype(bf16)
        grad_y = dot(x_out_ref[...], u_ref[b, at, :], NT).astype(bf16)
        for q in range(2):
            fg_ref[b, q, 0:128, at] = proj[256 + 128 * q : 384 + 128 * q]
            fg_ref[b, q, 128:256, at] = grad_y[128 * q : 128 * q + 128]
        return dot(pblk_ref[...], proj[0:C], NN)

    def soften(b, c, logits):
        lo = c * LANES
        valid = (iota((1, LANES), 1) + (b * STEP + lo) < count * ROWS).astype(f32)
        for h in range(H):
            at = pl.ds(h * G, G)
            scale = LOG2E / jnp.full((1, LANES), temp_ref[h], f32)
            part = logits[G * h : G * h + G]
            top = jnp.max(part, axis=0, keepdims=True)
            ex = jnp.exp2((part - top) * scale)
            wt = ex * (valid / jnp.sum(ex, axis=0, keepdims=True))
            w_ref[b, at, lo : lo + LANES] = wt.astype(bf16)

    @pl.loop(0, steps, step=UNROLL)
    def _(i):
        order = [(i + k, c) for k in range(UNROLL) for c in range(CHUNKS)]
        for k in range(UNROLL):
            for copy in rows_copies(i + k):
                copy.wait()
        logits = project(*order[0])
        for k, (b, c) in enumerate(order):
            following = project(*order[k + 1]) if k + 1 < len(order) else None
            soften(b, c, logits)
            logits = following
            if c == CHUNKS - 1:
                for q in range(2):
                    at = pl.ds(256 * q, 256)
                    acc_ref[q] += dot(fg_ref[b, q], w_ref[b, at, :], NT)

    @pl.loop(steps, STEPS)
    def _(b):
        for copy in rows_copies(b):
            copy.wait()

    core = lax.axis_index("grp")
    for q in range(2):
        raw = gather_heads(acc_ref[q, 0:128, :].T)
        grad = gather_heads(acc_ref[q, 128:256, :].T)
        norm = acc_ref[q, C : C + 8, :]
        row = iota((8, 128), 0)
        norm = jnp.where(row == 0, norm[:, 0:128], jnp.where(row == 1, norm[:, 128:256], 0.0))

        def put(ref):
            ref[0:64, :] = raw
            ref[64:128, :] = grad
            ref[128:136, :] = norm

        pl.when(core == q)(lambda: put(keep_ref))
        pl.when(core != q)(lambda: put(send_ref))


def first_sweep(x, u, region, tally, lut, e_in, x_out, part, temp):
    return pl.pallas_call(
        first_kernel,
        in_specs=[in_hbm()] * 9,
        out_specs=[in_vmem()] * 7,
        scratch_shapes=[
            pltpu.SMEM((2, 64), jnp.int32),
            pltpu.VMEM((2, BLOCKS, 64), jnp.int32),
            pltpu.SMEM((H,), f32),
            pltpu.VMEM((STEPS, STEP, C), bf16),
            pltpu.VMEM((PATCHES, C), bf16),
            pltpu.VMEM((C, 2 * C), bf16),
            pltpu.VMEM((C, C), bf16),
            pltpu.VMEM((D, G), bf16),
            pltpu.VMEM((2 * C, C), bf16),
            pltpu.VMEM((BLOCKS, C), f32),
            pltpu.VMEM((2, EXT, 256), f32),
            pltpu.SemaphoreType.DMA((STEPS,)),
            pltpu.SemaphoreType.DMA((STEPS,)),
            pltpu.SemaphoreType.DMA((7,)),
        ],
        out_shape=[
            pltpu.VMEM((STEPS, HG, STEP), bf16),
            pltpu.VMEM((STEPS, 2, EXT, STEP), bf16),
            pltpu.VMEM((STEPS, EXT, STEP), bf16),
            pltpu.VMEM((STEPS, STEP, C), bf16),
            jax.ShapeDtypeStruct((SUMS, 128), f32),
            jax.ShapeDtypeStruct((SUMS, 128), f32),
            jax.ShapeDtypeStruct((HG, C), bf16),
        ],
        compiler_params=pltpu.CompilerParams(vmem_limit_bytes=VMEM_LIMIT),
        name="first_sweep",
    )(*map(hbm, (tally, region, x, u, lut, e_in, x_out, part, temp)))


def xin_moment_kernel(lo, hi, tally_ref, xt_ref, w_ref, out_ref):
    out_ref[...] = jnp.zeros_like(out_ref)

    @pl.loop(lo, jnp.minimum(hi, step_count(tally_ref)))
    def _(b):
        out_ref[...] += dot(xt_ref[b], w_ref[b], NT)


def u_moment_kernel(lo, hi, tally_ref, u_ref, w_ref, out_ref):
    out_ref[...] = jnp.zeros_like(out_ref)

    @pl.loop(lo, jnp.minimum(hi, step_count(tally_ref)))
    def _(b):
        out_ref[...] += dot(w_ref[b], u_ref[b], NN)


def moment(kernel, shape, lo, hi, tally, rows, w):
    return pl.pallas_call(
        functools.partial(kernel, lo, hi),
        in_specs=[in_smem(), in_vmem(), in_vmem()],
        out_specs=in_vmem(),
        out_shape=pltpu.VMEM(shape, f32),
        compiler_params=SMALL,
        cost_estimate=pl.CostEstimate(
            flops=2 * (hi - lo) * STEP * HG * C, bytes_accessed=(hi - lo) * 2**20, transcendentals=0
        ),
        name="moment",
    )(tally, vmem(rows), vmem(w))


def middle_kernel(s_ref, t_ref, out_ref):
    raw = s_ref[0:64, :]
    grad = s_ref[64:128, :]
    norm = jnp.concatenate([s_ref[128:136, :], jnp.zeros((120, 128), f32)], axis=0).T
    denom = jnp.full((G, 128), EPS, f32)
    for j in range(4):
        col = norm[G * (j % 2) : G * (j % 2) + G, j // 2 : j // 2 + 1]
        denom = denom + jnp.where(head_mask(j, G), col, 0.0)
    inv = 1.0 / denom
    token = raw * inv
    t2 = (iota((D, 128), 0) == (iota((D, 128), 1) & (D - 1))).astype(f32).astype(bf16)
    own = (iota((128, 128), 0) >> 5) == (iota((128, 128), 1) >> 5)
    triple = t_ref[...]

    def diagonal(k):
        wide = dot(triple[:, D * k : D * k + D], t2, NN)
        return jnp.where(own, jnp.concatenate([wide] * 4, axis=0), 0.0).astype(bf16)

    wq, wk, wv = diagonal(0), diagonal(1), diagonal(2)
    query = dot_left2(token, wq, NN)
    keys = dot_left2(token, wk, NN)
    values = dot_left2(token, wv, NN)
    rate = 1.0 / math.sqrt(D)
    query_s = spread(query)
    scores = dot3(query_s, keys, NT) * rate
    scores = jnp.exp(scores - jnp.max(scores, axis=1, keepdims=True))
    probs = scores / jnp.sum(scores, axis=1, keepdims=True)
    out = gather_heads(dot3(probs, values, NN))
    grad_s = spread(grad)
    d_values = dot3(probs.T, grad_s, NN)
    d_probs = dot3(grad_s, values, NT)
    d_scores = probs * (d_probs - jnp.sum(d_probs * probs, axis=1, keepdims=True)) * rate
    d_query = gather_heads(dot3(d_scores, keys, NN))
    d_keys = dot3(d_scores.T, query_s, NN)
    d_token = (
        dot_left2(d_query, wq, NT) + dot_left2(d_keys, wk, NT) + dot_left2(d_values, wv, NT)
    )
    grad_raw = d_token * inv
    group = ((iota((128, 128), 0) >> 5) == iota((128, 128), 1)).astype(f32)
    first = (iota((128, 128), 1) < 4).astype(f32)
    grad_norm = -dot_left2(d_token * token * inv, (group * first).astype(bf16), NN)
    out_ref[0:64, :] = out.astype(bf16).astype(f32)
    out_ref[64:128, :] = grad_raw.astype(bf16).astype(f32)
    out_ref[128:192, :] = grad_norm
    token_t = jnp.concatenate([token, jnp.zeros((64, 128), f32)], axis=0).T[:, 0:64]
    total = jnp.zeros((D, 128), f32)
    for k, d_part in enumerate((d_query, d_keys, d_values)):
        full = jnp.where(own, dot3(token_t, d_part, NN), 0.0)
        full = full[0:32] + full[32:64] + (full[64:96] + full[96:128])
        fold = ((iota((128, 128), 0) & (D - 1)) + D * k == iota((128, 128), 1)).astype(f32)
        total = total + dot_left2(full, fold.astype(bf16), NN)
    out_ref[192:224, :] = total


def middle(sums, triple):
    return pl.pallas_call(
        middle_kernel,
        out_shape=jax.ShapeDtypeStruct((MID, 128), f32),
        compiler_params=SMALL,
        name="middle",
    )(sums, triple)


def second_kernel(
    tally_ref,
    region_ref,
    temp_ref,
    temp_row_ref,
    xt_ref,
    w_ref,
    fg_ref,
    mine_ref,
    theirs_ref,
    e_in_ref,
    pblk_ref,
    p_ref,
    y1_ref,
    y2_ref,
    z1_ref,
    z2_ref,
    gs_ref,
    pq_ref,
    keep_ref,
    send_ref,
    og_ref,
    gn_ref,
    v_ref,
    ob_ref,
    gr_ref,
    buf_ref,
):
    steps = step_count(tally_ref)
    core = lax.axis_index("grp")

    def prologue():
        for q in range(2):
            at = pl.ds(256 * q, 256)
            mine = core == q
            out_b = jnp.where(mine, mine_ref[0:64, :], theirs_ref[0:64, :])
            grad_raw = jnp.where(mine, mine_ref[64:128, :], theirs_ref[64:128, :])
            grad_norm = jnp.where(mine, mine_ref[128:192, :], theirs_ref[128:192, :])
            grad_norm = grad_norm - jnp.mean(grad_norm, axis=0, keepdims=True)
            for j in range(4):
                gn_ref[pl.ds(256 * q + G * j, G), :] = jnp.broadcast_to(
                    grad_norm[:, j : j + 1], (G, 128)
                ) / jnp.full((1, 128), temp_ref[4 * q + j], f32)
            cols = pl.ds(128 * q, 128)
            off = slice(0, 256) if q else slice(256, 512)
            zero = jnp.zeros((256, 128), bf16)
            ob_ref[at, cols] = spread(out_b).astype(bf16)
            gr_ref[at, cols] = spread(grad_raw).astype(bf16)
            ob_ref[off, cols] = zero
            gr_ref[off, cols] = zero
            sharp = jnp.full((1, 128), temp_ref[4 * q], f32)
            for j in range(1, 4):
                sharp = jnp.where(head_mask(j, 1), temp_ref[4 * q + j], sharp)
            og_ref[at, 0:128] = spread(
                (grad_raw - jnp.mean(grad_raw, axis=0, keepdims=True)) / sharp
            ).astype(bf16)
            og_ref[at, 128:256] = spread(
                (out_b - jnp.mean(out_b, axis=0, keepdims=True)) / sharp
            ).astype(bf16)
        v_ref[...] = jnp.zeros_like(v_ref)

    prologue()

    def grad_weights(b, c):
        at = [pl.ds(256 * q, 256) for q in range(2)]
        lanes = pl.ds(c * LANES, LANES)
        return [dot(og_ref[at[q], :], fg_ref[b, q, 0:C, lanes], NN) for q in range(2)]

    def grad_slices(b, c, grad_w):
        lanes = pl.ds(c * LANES, LANES)
        for h in range(H):
            at = pl.ds(h * G, G)
            col = jnp.concatenate([gn_ref[at, :]] * (LANES // 128), axis=1)
            j = G * (h & 3)
            wt = w_ref[b, at, lanes].astype(f32)
            wg = wt * (grad_w[h >> 2][j : j + G] + col)
            gs = wg - wt * jnp.sum(wg, axis=0, keepdims=True)
            gs_ref[b, at, lanes] = gs.astype(bf16)

    @pl.loop(0, steps, step=UNROLL)
    def _(i):
        order = [(i + k, c) for k in range(UNROLL) for c in range(CHUNKS)]
        grad_w = grad_weights(*order[0])
        for k, (b, c) in enumerate(order):
            following = grad_weights(*order[k + 1]) if k + 1 < len(order) else None
            grad_slices(b, c, grad_w)
            grad_w = following
            if c == CHUNKS - 1:
                v_ref[...] += dot(xt_ref[b], gs_ref[b], NT)

    v = v_ref[...]
    y = y1_ref[...] + y2_ref[...]
    pblk = pblk_ref[...]
    gr = gr_ref[...]
    pq_ref[:, 0:512] = dot(e_in_ref[:, 0:256], pblk, NT).astype(bf16)
    pq_ref[:, 512:1024] = dot(e_in_ref[:, 256:512], gr, NT).astype(bf16)
    buf_ref[0:256, :] = dot_left2(v[0:C], pblk, NN)
    buf_ref[256:512, :] = dot_left2(y[0:C], gr, NN)
    buf_ref[512:768, :] = dot_right2(ob_ref[...].astype(f32).T.astype(bf16), z1_ref[...] + z2_ref[...], NN)
    onehot = patch_onehot(region_ref).T.astype(bf16)
    per_block = dot_left2(v[C:EXT], pq_ref[:, 0:512], NT)
    per_block = per_block + dot_left2(y[C:EXT], pq_ref[:, 512:1024], NT)
    buf_ref[768:1280, :] = dot_right2(onehot, per_block, NN)
    et = e_in_ref[:, 0:256].T
    cross = dot_right2(et, v[0:C], NN)
    own = (iota((256, 512), 0) >> 5) == (iota((256, 512), 1) >> 6)
    cross = jnp.where(own, cross, 0.0)
    heads = cross[0:32]
    for k in range(1, 8):
        heads = heads + cross[32 * k : 32 * k + 32]
    by_slice = (heads[:, 0:128] + heads[:, 128:256]) + (heads[:, 256:384] + heads[:, 384:512])
    by_slice = by_slice + pltpu.roll(by_slice, G, 1)
    tile = (iota((G, HG), 0) == (iota((G, HG), 1) & (G - 1))).astype(f32).astype(bf16)
    by_head = ((iota((HG, 8), 0) >> 6) == iota((HG, 8), 1)).astype(f32).astype(bf16)
    weighed = heads * dot(p_ref[...], tile, NN)
    weighed = jnp.broadcast_to(jnp.sum(weighed, axis=0, keepdims=True), (8, HG))
    hi, mid, lo = split3(weighed)
    sharp = dot(hi, by_head, NN) + (dot(mid, by_head, NN) + dot(lo, by_head, NN))
    sharp = -sharp / temp_row_ref[...]
    buf_ref[1280:BUF, :] = jnp.zeros((BUF - 1280, 256), f32)
    buf_ref[1280:1312, 0:128] = by_slice
    buf_ref[1312:1320, 0:8] = sharp
    keep_ref[...] = buf_ref[pl.ds(pl.multiple_of(core * HALF, 16), HALF), :]
    send_ref[...] = buf_ref[
        pl.ds(pl.multiple_of((1 - core) * HALF, 16), HALF), :
    ].astype(bf16)


def second_sweep(tally, region, temp, xt, w, fg, mine, theirs, e_in, pblk, part, *moments):
    return pl.pallas_call(
        second_kernel,
        in_specs=[in_smem(), in_vmem(), in_smem()] + [in_vmem()] * 13,
        out_specs=[in_vmem()] * 4,
        scratch_shapes=[
            pltpu.VMEM((HG, 256), bf16),
            pltpu.VMEM((HG, 128), f32),
            pltpu.VMEM((EXT, HG), f32),
            pltpu.VMEM((HG, C), bf16),
            pltpu.VMEM((HG, C), bf16),
            pltpu.VMEM((BUF, C), f32),
        ],
        out_shape=[
            pltpu.VMEM((STEPS, HG, STEP), bf16),
            pltpu.VMEM((C, 1024), bf16),
            pltpu.VMEM((HALF, C), f32),
            pltpu.VMEM((HALF, C), bf16),
        ],
        compiler_params=pltpu.CompilerParams(vmem_limit_bytes=VMEM_LIMIT),
        name="second_sweep",
    )(
        tally, region, temp, temp.reshape(1, H), vmem(xt), vmem(w), vmem(fg), mine, theirs,
        e_in, pblk, part, *map(vmem, moments),
    )


def points_kernel(first, number, tally_ref, gs_ref, w_ref, pq_ref, *refs):
    out_hbm, out_ref, sem = refs[-3:]
    steps = step_count(tally_ref)

    def copy(k):
        at = pl.ds(pl.multiple_of((first + k) * STEP, STEP), STEP)
        return pltpu.make_async_copy(out_ref.at[k], out_hbm.at[at, :], sem.at[k])

    @pl.loop(0, number)
    def _(k):
        b = first + k

        @pl.when(b < steps)
        def _():
            grad = dot(pq_ref[:, 0:512], gs_ref[b], NN) + dot(pq_ref[:, 512:1024], w_ref[b], NN)
            out_ref[k] = grad.T.astype(bf16)

        @pl.when(b >= steps)
        def _():
            out_ref[k] = jnp.zeros((STEP, C), bf16)

        copy(k).start()

    @pl.loop(0, number)
    def _(k):
        copy(k).wait()


def points(tally, gs, w, pq, first, number, into=None):
    more = () if into is None else (into,)
    return pl.pallas_call(
        functools.partial(points_kernel, first, number),
        in_specs=[in_smem(), in_vmem(), in_vmem(), in_vmem()] + [in_hbm()] * len(more),
        out_specs=in_hbm(),
        out_shape=pltpu.HBM((BLOCKS * ROWS, C), bf16),
        scratch_shapes=[pltpu.VMEM((number, STEP, C), bf16), pltpu.SemaphoreType.DMA((number,))],
        input_output_aliases={4: 0} if more else {},
        compiler_params=SMALL,
        cost_estimate=pl.CostEstimate(
            flops=4 * number * STEP * HG * C, bytes_accessed=number * 2**20, transcendentals=0
        ),
        name="points",
    )(tally, vmem(gs), vmem(w), vmem(pq), *map(hbm, more))


def pieces_kernel(keep_ref, recv_ref, own_ref, p1_ref, p2_ref, p3_ref):
    z = ring_place(lax.axis_index("grp"))

    def piece(k):
        at = pl.ds(pl.multiple_of((z ^ k) * PIECE, 16), PIECE)
        return keep_ref[at, :] + recv_ref[at, :].astype(f32)

    own_ref[...] = piece(0)
    p1_ref[...] = piece(1).astype(bf16)
    p2_ref[...] = piece(2).astype(bf16)
    p3_ref[...] = piece(3).astype(bf16)


def pieces(keep, recv):
    spec = in_vmem()
    return pl.pallas_call(
        pieces_kernel,
        in_specs=[spec, spec],
        out_specs=[spec] * 4,
        out_shape=[jax.ShapeDtypeStruct((PIECE, C), f32)]
        + [jax.ShapeDtypeStruct((PIECE, C), bf16)] * 3,
        compiler_params=SMALL,
        name="pieces",
    )(vmem(keep), recv)


def final_kernel(mine_ref, theirs_ref, patch_ref, win_ref, slice_ref, temp_ref, wout_ref, buf_ref):
    core = lax.axis_index("grp")
    for ref, half in ((mine_ref, core), (theirs_ref, 1 - core)):
        z = ring_place(half)
        for k in range(4):
            at = pl.multiple_of(half * HALF + (z ^ k) * PIECE, 16)
            buf_ref[pl.ds(at, PIECE), :] = ref[k]
    win_ref[:, 0:256] = buf_ref[0:256, :].astype(f32)
    win_ref[:, 256:512] = buf_ref[256:512, :].astype(f32)
    wout_ref[...] = buf_ref[512:768, :].astype(f32)
    patch_ref[...] = buf_ref[768:1280, :].astype(f32)
    slice_ref[...] = buf_ref[1280:1312, 0:64].astype(f32)
    temp_ref[...] = buf_ref[1312:1328, 0:8].astype(f32)[0:1, :]


def final(mine, theirs):
    spec = in_vmem()
    return pl.pallas_call(
        final_kernel,
        in_specs=[spec, spec],
        out_specs=[spec] * 5,
        out_shape=[
            jax.ShapeDtypeStruct((PATCHES, C), f32),
            jax.ShapeDtypeStruct((C, 2 * C), f32),
            jax.ShapeDtypeStruct((D, G), f32),
            jax.ShapeDtypeStruct((1, H), f32),
            jax.ShapeDtypeStruct((C, C), f32),
        ],
        scratch_shapes=[pltpu.VMEM((BUF, C), bf16)],
        compiler_params=SMALL,
        name="final",
    )(mine, theirs)


def shift_pairs(step, k):
    pairs = []
    for device in range(128):
        unit = UNITS[AXES[device % 2][step]] * 2
        at = (device // unit) % 4
        pairs.append((device, device + ((at ^ k) - at) * unit))
    return pairs


def shift(v, step, k):
    return lax.ppermute(v, ("pts", "grp"), shift_pairs(step, k))


def swap(v):
    return lax.ppermute(v, "grp", [(0, 1), (1, 0)])


def ring_sum(v, step):
    one, three, two = shift(v, step, 1), shift(v, step, 3), shift(v, step, 2)
    return (v + two) + (one + three)


def ring_sum_b(v, step):
    sent = v.astype(bf16)
    one, three, two = (shift(sent, step, k).astype(f32) for k in (1, 3, 2))
    return lax.reduce_precision((v + two) + (one + three), 8, 7)


def shards(x, u, region, tally, lut, e_in, part, temp, triple, x_out):
    tally, region = tally.T, region.transpose(1, 2, 0)
    w, fg, xt, u_kept, keep, send, pblk = first_sweep(
        x, u, region, tally, lut, e_in, x_out, part, temp
    )
    sums = keep + swap(send)
    third = STEPS // 4
    sums = ring_sum(sums, 0)
    y1 = moment(xin_moment_kernel, (EXT, HG), 0, STEPS - third, tally, xt, w)
    sums, y1 = lax.optimization_barrier((sums, y1))
    sums = ring_sum(sums, 1)
    y2 = moment(xin_moment_kernel, (EXT, HG), STEPS - third, STEPS, tally, xt, w)
    z1 = moment(u_moment_kernel, (HG, C), 0, third, tally, u_kept, w)
    sums, y2, z1 = lax.optimization_barrier((sums, y2, z1))
    sums = ring_sum(sums, 2)
    z2 = moment(u_moment_kernel, (HG, C), third, STEPS, tally, u_kept, w)
    sums, z2 = lax.optimization_barrier((sums, z2))
    mine = middle(sums, triple)
    theirs = swap(mine)
    w_qkv = (mine[192:224] + theirs[192:224])[:, 0:96]

    gs, pq, keep, send = second_sweep(
        tally, region, temp, xt, w, fg, mine, theirs, e_in, pblk, part, y1, y2, z1, z2
    )
    own, p1, p2, p3 = pieces(keep, swap(send))
    part_steps = STEPS // 4

    def rows_beside(total, done, k):
        done = points(tally, gs, w, pq, k * part_steps, part_steps, done)
        return lax.optimization_barrier((total, done))

    r1, r2, r3 = shift(p1, 0, 1), shift(p2, 0, 2), shift(p3, 0, 3)
    total = (own + r1.astype(f32)) + (r2.astype(f32) + r3.astype(f32))
    total = lax.reduce_precision(total, 8, 7)
    total, grad_points = rows_beside(total, None, 0)
    total = ring_sum_b(total, 1)
    total, grad_points = rows_beside(total, grad_points, 1)
    total = ring_sum_b(total, 2)
    total, grad_points = rows_beside(total, grad_points, 2)
    mine = total.astype(bf16)
    mine = jnp.stack([mine] + [shift(mine, 0, k) for k in (1, 2, 3)])
    mine, grad_points = rows_beside(mine, grad_points, 3)
    patch, w_in, w_slice, w_temp, w_out = final(mine, swap(mine))
    return grad_points, patch, w_in, w_slice, w_temp.reshape(H), w_qkv, w_out


def solution(mesh):
    rows = P(("pts", "grp"), None)
    return jax.shard_map(
        shards,
        mesh=mesh,
        in_specs=(rows, rows) + (P(),) * 8,
        out_specs=(rows,) + (P(),) * 6,
        check_vma=False,
    )
```

time: 114 us -> 99.7 us (0.87)
  waiting for transfers between devices: 21.2 us -> 5.32 us
  Pallas kernels: 38.3 us -> 51.1 us
  starting transfers between devices: 48.2 us -> 40.8 us
  local copies, waits for them, and re-layouts: 3.37 us -> 0.04 us
    ppermute x21, waiting for transfers between devices: 16.6 us -> 1.46 us  [shift(): return lax.ppermute(v, ('pts', 'grp'), shift_pairs(step, k))]
    ppermute x21, starting transfers between devices: 39 us -> 28 us  [shift(): return lax.ppermute(v, ('pts', 'grp'), shift_pairs(step, k))]
    pallas_call x3 -> x5, Pallas kernels: 16 us -> 25.2 us  [the longest x1 15.4 us: first_sweep(): pl.pallas_call(first_kernel, in_specs=[in_hbm()] * 9, out_specs=[in_vmem(...]
    pallas_call x2 -> x4, Pallas kernels: 7.56 us -> 11.8 us  [points(): pl.pallas_call(functools.partial(points_kernel, first, number), in_specs=...]
    ppermute x4, starting transfers between devices: 9.2 us -> 12.8 us  [swap(): return lax.ppermute(v, 'grp', [(0, 1), (1, 0)])]
    unnamed x18 -> x12, local copies, waits for them, and re-layouts: 3.37 us -> 0.04 us
    pallas_call x1, Pallas kernels: 3.58 us -> 2.3 us  [middle(): pl.pallas_call(middle_kernel, out_shape=jax.ShapeDtypeStruct((MID, 128),...]
  transfers between devices with their start and end apart: 25 -> 25, of which waited for: 15 -> 7; matrix products, arithmetic and copies ran while one was open for 1% -> 1% of each run, Pallas kernels for 12% -> 22%
where the time goes in v2:
time: 99.7 us; the launch traced here: 99.2 us
  Pallas kernels  51.1 us (51%)
  starting transfers between devices  40.8 us (41%)
  waiting for transfers between devices  5.32 us (5%)
  between operations  1.02 us (1%)
    ppermute x21, starting transfers between devices, shift(): return lax.ppermute(v, ('pts', 'grp'), shift_pairs(step, k))  28 us
    pallas_call x1, Pallas kernels, first_sweep(): pl.pallas_call(first_kernel, in_specs=[in_hbm()] * 9, out_specs=[in_vmem(...  15.4 us
    ppermute x4, starting transfers between devices, swap(): return lax.ppermute(v, 'grp', [(0, 1), (1, 0)])  12.8 us
    pallas_call x4, Pallas kernels, points(): pl.pallas_call(functools.partial(points_kernel, first, number), in_specs=...  11.8 us
    pallas_call x1, Pallas kernels, second_sweep(): pl.pallas_call(second_kernel, in_specs=[in_smem(), in_vmem(), in_smem()]...  10.6 us
    pallas_call x4, Pallas kernels, moment(): pl.pallas_call(functools.partial(kernel, lo, hi), in_specs=[in_smem(), in...  9.8 us
    ppermute x4, waiting for transfers between devices, swap(): return lax.ppermute(v, 'grp', [(0, 1), (1, 0)])  3.86 us
    pallas_call x1, Pallas kernels, middle(): pl.pallas_call(middle_kernel, out_shape=jax.ShapeDtypeStruct((MID, 128),...  2.3 us
  transfers between devices with their start and end apart: 25, of which 7 were waited for; matrix products, arithmetic and copies ran while one was open for 1% of the time, Pallas kernels for 22%

profile of v2, /device:TPU:1, one launch (start us, length us, event | category | flops | bytes accessed | tf_op | source)
XLA Modules:
  0.0 99.2 jit_solution(17863142153843370948)
XLA Ops:
  0.6 15.4 %first_sweep.1 = (bf16[8,512,1024]{2,1,0:T(8,128)(2,1)S(1)}, bf16[8,2,272,1024]{3,2,1,0:T(8,128)(2,1)S(1)}, bf16[8,272,1024]{2,1,0:T(8,128)(2,1)S(1)}, bf16[8,10...) custom-call(s32[2,64]{1,0:T(2,128)} %bitcast.8, ...), custom_call_target="tpu_custom_call" | custom-call | tf_op jit(solution)/shard_map/first_sweep/pallas_call | solution.py:282
  16.0 1.5 %collective-permute-start = (f32[136,128]{1,0:T(8,128)S(1)}, f32[136,128]{1,0:T(8,128)S(1)}, u32[]{:S(2)}, u32[]{:S(2)}) collective-permute-start(f32[136,128]{1,0:T(8,128)S(1)} %get-tuple-element.46), channel_id=1, source_target_pairs={{0,1},{1,0},{2,3},{3,2},{4,5},{5,4},{6,7},{7,6},{8,9},{9,8},{10,11... | collective-permute-start | bytes 208904 | tf_op jit(solution)/shard_map/ppermute | solution.py:683
  17.5 0.9 collective-permute-done
  18.4 3.1 %collective-permute-start.1 = (f32[136,128]{1,0:T(8,128)S(1)}, f32[136,128]{1,0:T(8,128)S(1)}, u32[]{:S(2)}, u32[]{:S(2)}) collective-permute-start(f32[136,128]{1,0:T(8,128)S(1)} %add.60), channel_id=1, source_target_pairs={{0,4},{1,17},{2,6},{3,19},{4,0},{5,21},{6,2},{7,23},{8,12},{9,25},... | collective-permute-start | bytes 208904 | tf_op jit(solution)/shard_map/ppermute | solution.py:679
  21.5 0.4 collective-permute-start.2
  21.9 0.4 collective-permute-start.3
  22.3 3.5 %moment.4.y1_ref = f32[272,512]{1,0:T(8,128)S(1)} custom-call(s32[2,64]{1,0:T(2,128)S(1)} %bitcast.9, bf16[8,272,1024]{2,1,0:T(8,128)(2,1)S(1)} %get-tuple-element.42.xt_ref, bf16[8,512,1024]{2,1,0:T(8,128)(2,1)S(1)} %get-tuple-element.43.w_ref), custom_call_target="tpu_custom_call" | custom-call | flops 1610612736 | bytes 6291456 | tf_op jit(solution)/shard_map/moment/pallas_call | solution.py:333
  25.8 0.0 collective-permute-done.1
  25.8 0.4 collective-permute-done.3
  26.3 0.1 collective-permute-start.4
  26.4 0.1 collective-permute-start.5
  26.5 3.1 %collective-permute-start.6 = (f32[136,128]{1,0:T(8,128)S(1)}, f32[136,128]{1,0:T(8,128)S(1)}, u32[]{:S(2)}, u32[]{:S(2)}) collective-permute-start(f32[136,128]{1,0:T(8,128)S(1)} %add_add_fusion.2), channel_id=1, source_target_pairs={{0,24},{1,97},{2,26},{3,99},{4,28},{5,101},{6,30},{7,103},{8,16},{... | collective-permute-start | bytes 208904 | tf_op jit(solution)/shard_map/ppermute | solution.py:679
  29.6 1.6 %moment.5.y2_ref = f32[272,512]{1,0:T(8,128)S(1)} custom-call(s32[2,64]{1,0:T(2,128)S(1)} %bitcast.10, bf16[8,272,1024]{2,1,0:T(8,128)(2,1)S(1)} %get-tuple-element.42.xt_ref, bf16[8,512,1024]{2,1,0:T(8,128)(2,1)S(1)} %get-tuple-element.43.w_ref), custom_call_target="tpu_custom_call" | custom-call | flops 536870912 | bytes 2097152 | tf_op jit(solution)/shard_map/moment/pallas_call | solution.py:333
  31.2 1.5 %moment.6.z1_ref = f32[512,256]{1,0:T(8,128)S(1)} custom-call(s32[2,64]{1,0:T(2,128)S(1)} %bitcast.11, bf16[8,1024,256]{2,1,0:T(8,128)(2,1)S(1)} %get-tuple-element.48.u_ref, bf16[8,512,1024]{2,1,0:T(8,128)(2,1)S(1)} %get-tuple-element.43.w_ref), custom_call_target="tpu_custom_call" | custom-call | flops 536870912 | bytes 2097152 | tf_op jit(solution)/shard_map/moment/pallas_call | solution.py:333
  32.7 0.0 collective-permute-done.4
  32.7 0.0 collective-permute-done.5
  32.7 0.0 copy-start.4
  32.8 0.0 copy-start
  32.8 0.0 copy-start.2
  32.8 0.0 copy-start.3
  32.8 0.0 copy-start.5
  32.8 4.8 %collective-permute-start.7 = (f32[136,128]{1,0:T(8,128)S(1)}, f32[136,128]{1,0:T(8,128)S(1)}, u32[]{:S(2)}, u32[]{:S(2)}) collective-permute-start(f32[136,128]{1,0:T(8,128)S(1)} %add_add_fusion.1), channel_id=1, source_target_pairs={{0,64},{1,5},{2,66},{3,7},{4,68},{5,1},{6,70},{7,3},{8,72},{9,13},... | collective-permute-start | bytes 208904 | tf_op jit(solution)/shard_map/ppermute | solution.py:679
  37.6 0.7 collective-permute-start.8
  38.3 0.8 collective-permute-start.9
  39.1 3.3 %moment.7.z2_ref = f32[512,256]{1,0:T(8,128)S(1)} custom-call(s32[2,64]{1,0:T(2,128)S(1)} %bitcast.12, bf16[8,1024,256]{2,1,0:T(8,128)(2,1)S(1)} %get-tuple-element.48.u_ref, bf16[8,512,1024]{2,1,0:T(8,128)(2,1)S(1)} %get-tuple-element.43.w_ref), custom_call_target="tpu_custom_call" | custom-call | flops 1610612736 | bytes 6291456 | tf_op jit(solution)/shard_map/moment/pallas_call | solution.py:333
  42.4 0.0 collective-permute-done.8
  42.4 0.3 collective-permute-done.9
  42.7 2.3 %middle.1.mine_ref = f32[224,128]{1,0:T(8,128)S(1)} custom-call(f32[136,128]{1,0:T(8,128)S(1)} %add_add_fusion.s_ref, bf16[32,96]{1,0:T(8,128)(2,1)S(1)} %copy-done.4), custom_call_target="tpu_custom_call" | custom-call | tf_op jit(solution)/shard_map/middle/pallas_call | solution.py:401
  45.0 5.5 %collective-permute-start.10 = (f32[224,128]{1,0:T(8,128)S(1)}, f32[224,128]{1,0:T(8,128)S(1)}, u32[]{:S(2)}, u32[]{:S(2)}) collective-permute-start(f32[224,128]{1,0:T(8,128)S(1)} %middle.1.mine_ref), channel_id=1, source_target_pairs={{0,1},{1,0},{2,3},{3,2},{4,5},{5,4},{6,7},{7,6},{8,9},{9,8},{10,11... | collective-permute-start | bytes 344072 | tf_op jit(solution)/shard_map/ppermute | solution.py:683
  50.5 1.0 collective-permute-done.10.theirs_ref
  51.5 10.6 %second_sweep.1 = (bf16[8,512,1024]{2,1,0:T(8,128)(2,1)S(1)}, bf16[256,1024]{1,0:T(8,128)(2,1)S(1)}, f32[704,256]{1,0:T(8,128)S(1)}, bf16[704,256]{1,0:T(8,128)(2,1)S(1)}) custom-call(s32[2,64]{1,0:T(2,128)S(1)} %bitcast.13, s32[2,16,64]{2,1,0:T(8,128)S(1)} %bitcast.19, f32[8]{0:T(128)S(1)} %copy-done.5, f32[1,8]{1,0:T(1,128)S(1)} %bitcast.20, ...), custom_call_target="tpu_custom_call" | custom-call | tf_op jit(solution)/shard_map/second_sweep/pallas_call | solution.py:538
  62.0 0.4 collective-permute-start.11
  62.5 1.3 %collective-permute-done.11.recv_ref = bf16[704,256]{1,0:T(8,128)(2,1)S(1)} collective-permute-done((bf16[704,256]{1,0:T(8,128)(2,1)S(1)}, bf16[704,256]{1,0:T(8,128)(2,1)S(1)}, u32[]{:S(2)}, u32[]{:S(2)}) %collective-permute-start.11) | collective-permute-done | bytes 360480 | tf_op jit(solution)/shard_map/ppermute | solution.py:683
  63.8 0.1 pieces.1
  63.9 0.1 collective-permute-start.12
  64.0 1.1 %collective-permute-start.13 = (bf16[176,256]{1,0:T(8,128)(2,1)S(1)}, bf16[176,256]{1,0:T(8,128)(2,1)S(1)}, u32[]{:S(2)}, u32[]{:S(2)}) collective-permute-start(bf16[176,256]{1,0:T(8,128)(2,1)S(1)} %get-tuple-element.60), channel_id=1, source_target_pairs={{0,4},{1,17},{2,6},{3,19},{4,0},{5,21},{6,2},{7,23},{8,12},{9,25},... | collective-permute-start | bytes 270344 | tf_op jit(solution)/shard_map/ppermute | solution.py:679
  65.0 2.8 %collective-permute-start.14 = (bf16[176,256]{1,0:T(8,128)(2,1)S(1)}, bf16[176,256]{1,0:T(8,128)(2,1)S(1)}, u32[]{:S(2)}, u32[]{:S(2)}) collective-permute-start(bf16[176,256]{1,0:T(8,128)(2,1)S(1)} %get-tuple-element.61), channel_id=1, source_target_pairs={{0,6},{1,25},{2,4},{3,27},{4,2},{5,29},{6,0},{7,31},{8,14},{9,17},... | collective-permute-start | bytes 270344 | tf_op jit(solution)/shard_map/ppermute | solution.py:679
  67.8 3.0 %points.4.refs_0_ = bf16[8192,256]{1,0:T(8,128)(2,1)} custom-call(s32[2,64]{1,0:T(2,128)S(1)} %bitcast.14, bf16[8,512,1024]{2,1,0:T(8,128)(2,1)S(1)} %get-tuple-element.62.gs_ref, bf16[8,512,1024]{2,1,0:T(8,128)(2,1)S(1)} %get-tuple-element.43.w_ref, bf16[256,1024]{1,0:T(8,128)(2,1)S(1)} %get-tuple-element.63.pq_ref), custom_call_target="tpu_custom_call" | custom-call | flops 1073741824 | bytes 2097152 | tf_op jit(solution)/shard_map/points/pallas_call | solution.py:594
  70.8 0.0 collective-permute-done.13
  70.8 0.1 add_reduce-precision_fusion.2
  70.9 0.1 collective-permute-start.15
  71.0 0.1 collective-permute-start.16
  71.1 3.1 %collective-permute-start.17 = (bf16[176,256]{1,0:T(8,128)(2,1)S(1)}, bf16[176,256]{1,0:T(8,128)(2,1)S(1)}, u32[]{:S(2)}, u32[]{:S(2)}) collective-permute-start(bf16[176,256]{1,0:T(8,128)(2,1)S(1)} %convert_element_type.39), channel_id=1, source_target_pairs={{0,24},{1,97},{2,26},{3,99},{4,28},{5,101},{6,30},{7,103},{8,16},{... | collective-permute-start | bytes 270344 | tf_op jit(solution)/shard_map/ppermute | solution.py:679
  74.2 3.0 %points.5.refs_0_ = bf16[8192,256]{1,0:T(8,128)(2,1)} custom-call(s32[2,64]{1,0:T(2,128)S(1)} %bitcast.15, bf16[8,512,1024]{2,1,0:T(8,128)(2,1)S(1)} %get-tuple-element.62.gs_ref, bf16[8,512,1024]{2,1,0:T(8,128)(2,1)S(1)} %get-tuple-element.43.w_ref, bf16[256,1024]{1,0:T(8,128)(2,1)S(1)} %get-tuple-element.63.pq_ref, ...), custom_call_target="tpu_custom_call", output_to_operand_aliasing={{}: (4, {})} | custom-call | flops 1073741824 | bytes 2097152 | tf_op jit(solution)/shard_map/points/pallas_call | solution.py:594
  77.2 0.0 collective-permute-done.16
  77.2 0.0 collective-permute-done.17
  77.2 0.1 add_reduce-precision_fusion.1
  77.3 0.9 collective-permute-start.18
  78.2 0.7 collective-permute-start.19
  78.9 1.7 %collective-permute-start.20 = (bf16[176,256]{1,0:T(8,128)(2,1)S(1)}, bf16[176,256]{1,0:T(8,128)(2,1)S(1)}, u32[]{:S(2)}, u32[]{:S(2)}) collective-permute-start(bf16[176,256]{1,0:T(8,128)(2,1)S(1)} %convert_element_type.43), channel_id=1, source_target_pairs={{0,96},{1,7},{2,98},{3,5},{4,100},{5,3},{6,102},{7,1},{8,104},{9,1... | collective-permute-start | bytes 270344 | tf_op jit(solution)/shard_map/ppermute | solution.py:679
  80.6 3.0 %points.6.refs_0_ = bf16[8192,256]{1,0:T(8,128)(2,1)} custom-call(s32[2,64]{1,0:T(2,128)S(1)} %bitcast.16, bf16[8,512,1024]{2,1,0:T(8,128)(2,1)S(1)} %get-tuple-element.62.gs_ref, bf16[8,512,1024]{2,1,0:T(8,128)(2,1)S(1)} %get-tuple-element.43.w_ref, bf16[256,1024]{1,0:T(8,128)(2,1)S(1)} %get-tuple-element.63.pq_ref, ...), custom_call_target="tpu_custom_call", output_to_operand_aliasing={{}: (4, {})} | custom-call | flops 1073741824 | bytes 2097152 | tf_op jit(solution)/shard_map/points/pallas_call | solution.py:594
  83.6 0.0 collective-permute-done.19
  83.6 0.0 collective-permute-done.20
  83.7 0.1 collective-permute-start.21
  83.8 3.0 %collective-permute-start.22 = (bf16[176,256]{1,0:T(8,128)(2,1)S(1)}, bf16[176,256]{1,0:T(8,128)(2,1)S(1)}, u32[]{:S(2)}, u32[]{:S(2)}) collective-permute-start(bf16[176,256]{1,0:T(8,128)(2,1)S(1)} %add_reduce-precision_fusion), channel_id=1, source_target_pairs={{0,4},{1,17},{2,6},{3,19},{4,0},{5,21},{6,2},{7,23},{8,12},{9,25},... | collective-permute-start | bytes 270344 | tf_op jit(solution)/shard_map/ppermute | solution.py:679
  86.7 0.9 collective-permute-start.23
  87.6 3.0 %points.7 = bf16[8192,256]{1,0:T(8,128)(2,1)} custom-call(s32[2,64]{1,0:T(2,128)S(1)} %bitcast.17, bf16[8,512,1024]{2,1,0:T(8,128)(2,1)S(1)} %get-tuple-element.62.gs_ref, bf16[8,512,1024]{2,1,0:T(8,128)(2,1)S(1)} %get-tuple-element.43.w_ref, bf16[256,1024]{1,0:T(8,128)(2,1)S(1)} %get-tuple-element.63.pq_ref, ...), custom_call_target="tpu_custom_call", output_to_operand_aliasing={{}: (4, {})} | custom-call | flops 1073741824 | bytes 2097152 | tf_op jit(solution)/shard_map/points/pallas_call | solution.py:594
  90.6 0.0 collective-permute-done.21
  90.6 0.0 collective-permute-done.22
  90.6 0.7 collective-permute-done.23
  91.4 5.3 %collective-permute-start.24 = (bf16[4,176,256]{2,1,0:T(8,128)(2,1)S(1)}, bf16[4,176,256]{2,1,0:T(8,128)(2,1)S(1)}, u32[]{:S(2)}, u32[]{:S(2)}) collective-permute-start(bf16[4,176,256]{2,1,0:T(8,128)(2,1)S(1)} %pad_maximum_fusion.mine_ref), channel_id=1, source_target_pairs={{0,1},{1,0},{2,3},{3,2},{4,5},{5,4},{6,7},{7,6},{8,9},{9,8},{10,11... | collective-permute-start | bytes 1081352 | tf_op jit(solution)/shard_map/ppermute | solution.py:683
  96.7 0.6 slice_add_fusion
  97.3 0.7 collective-permute-done.24.theirs_ref
  98.0 1.2 %final.1 = (f32[512,256]{1,0:T(8,128)}, f32[256,512]{1,0:T(8,128)}, f32[32,64]{1,0:T(8,128)}, f32[1,8]{1,0:T(1,128)}, f32[256,256]{1,0:T(8,128)}) custom-call(bf16[4,176,256]{2,1,0:T(8,128)(2,1)S(1)} %pad_maximum_fusion.mine_ref, bf16[4,176,256]{2,1,0:T(8,128)(2,1)S(1)} %collective-permute-done.24.theirs_ref), custom_call_target="tpu_custom_call" | custom-call | tf_op jit(solution)/shard_map/final/pallas_call | solution.py:652
  (24 shorter events, 0.2 us)
Async XLA Ops:
  0.6 21.7 %copy-start.1 = (s32[64,2]{0,1:T(2,128)S(1)}, s32[64,2]{0,1:T(2,128)}, u32[]{:S(2)}) copy-start(s32[64,2]{0,1:T(2,128)} %param.13) | copy-start | bytes 1540
  16.0 2.4 %collective-permute-start = (f32[136,128]{1,0:T(8,128)S(1)}, f32[136,128]{1,0:T(8,128)S(1)}, u32[]{:S(2)}, u32[]{:S(2)}) collective-permute-start(f32[136,128]{1,0:T(8,128)S(1)} %get-tuple-element.46), channel_id=1, source_target_pairs={{0,1},{1,0},{2,3},{3,2},{4,5},{5,4},{6,7},{7,6},{8,9},{9,8},{10,11... | collective-permute-start | bytes 208904 | tf_op jit(solution)/shard_map/ppermute | solution.py:683
  18.4 7.4 %collective-permute-start.1 = (f32[136,128]{1,0:T(8,128)S(1)}, f32[136,128]{1,0:T(8,128)S(1)}, u32[]{:S(2)}, u32[]{:S(2)}) collective-permute-start(f32[136,128]{1,0:T(8,128)S(1)} %add.60), channel_id=1, source_target_pairs={{0,4},{1,17},{2,6},{3,19},{4,0},{5,21},{6,2},{7,23},{8,12},{9,25},... | collective-permute-start | bytes 208904 | tf_op jit(solution)/shard_map/ppermute | solution.py:679
  21.5 4.3 %collective-permute-start.2 = (f32[136,128]{1,0:T(8,128)S(1)}, f32[136,128]{1,0:T(8,128)S(1)}, u32[]{:S(2)}, u32[]{:S(2)}) collective-permute-start(f32[136,128]{1,0:T(8,128)S(1)} %add.60), channel_id=1, source_target_pairs={{0,2},{1,9},{2,0},{3,11},{4,6},{5,13},{6,4},{7,15},{8,10},{9,1},{1... | collective-permute-start | bytes 208904 | tf_op jit(solution)/shard_map/ppermute | solution.py:679
  21.9 4.4 %collective-permute-start.3 = (f32[136,128]{1,0:T(8,128)S(1)}, f32[136,128]{1,0:T(8,128)S(1)}, u32[]{:S(2)}, u32[]{:S(2)}) collective-permute-start(f32[136,128]{1,0:T(8,128)S(1)} %add.60), channel_id=1, source_target_pairs={{0,6},{1,25},{2,4},{3,27},{4,2},{5,29},{6,0},{7,31},{8,14},{9,17},... | collective-permute-start | bytes 208904 | tf_op jit(solution)/shard_map/ppermute | solution.py:679
  26.3 6.4 %collective-permute-start.4 = (f32[136,128]{1,0:T(8,128)S(1)}, f32[136,128]{1,0:T(8,128)S(1)}, u32[]{:S(2)}, u32[]{:S(2)}) collective-permute-start(f32[136,128]{1,0:T(8,128)S(1)} %add_add_fusion.2), channel_id=1, source_target_pairs={{0,16},{1,65},{2,18},{3,67},{4,20},{5,69},{6,22},{7,71},{8,24},{9,... | collective-permute-start | bytes 208904 | tf_op jit(solution)/shard_map/ppermute | solution.py:679
  26.4 6.3 %collective-permute-start.5 = (f32[136,128]{1,0:T(8,128)S(1)}, f32[136,128]{1,0:T(8,128)S(1)}, u32[]{:S(2)}, u32[]{:S(2)}) collective-permute-start(f32[136,128]{1,0:T(8,128)S(1)} %add_add_fusion.2), channel_id=1, source_target_pairs={{0,8},{1,33},{2,10},{3,35},{4,12},{5,37},{6,14},{7,39},{8,0},{9,41... | collective-permute-start | bytes 208904 | tf_op jit(solution)/shard_map/ppermute | solution.py:679
  26.5 6.2 %collective-permute-start.6 = (f32[136,128]{1,0:T(8,128)S(1)}, f32[136,128]{1,0:T(8,128)S(1)}, u32[]{:S(2)}, u32[]{:S(2)}) collective-permute-start(f32[136,128]{1,0:T(8,128)S(1)} %add_add_fusion.2), channel_id=1, source_target_pairs={{0,24},{1,97},{2,26},{3,99},{4,28},{5,101},{6,30},{7,103},{8,16},{... | collective-permute-start | bytes 208904 | tf_op jit(solution)/shard_map/ppermute | solution.py:679
  32.7 10.0 %copy-start.4 = (bf16[32,96]{1,0:T(8,128)(2,1)S(1)}, bf16[32,96]{1,0:T(8,128)(2,1)}, u32[]{:S(2)}) copy-start(bf16[32,96]{1,0:T(8,128)(2,1)} %t_ref.1) | copy-start | bytes 18436
  32.8 18.7 %copy-start = (bf16[256,512]{1,0:T(8,128)(2,1)S(1)}, bf16[256,512]{1,0:T(8,128)(2,1)}, u32[]{:S(2)}) copy-start(bf16[256,512]{1,0:T(8,128)(2,1)} %e_in_ref.1) | copy-start | bytes 786436
  32.8 18.7 %copy-start.2 = (s32[64,2,16]{0,2,1:T(8,128)S(1)}, s32[64,2,16]{0,2,1:T(8,128)}, u32[]{:S(2)}) copy-start(s32[64,2,16]{0,2,1:T(8,128)} %param.12) | copy-start | bytes 24580
  32.8 18.7 %copy-start.3 = (bf16[32,64]{1,0:T(8,128)(2,1)S(1)}, bf16[32,64]{1,0:T(8,128)(2,1)}, u32[]{:S(2)}) copy-start(bf16[32,64]{1,0:T(8,128)(2,1)} %p_ref.1) | copy-start | bytes 12292
  32.8 18.7 %copy-start.5 = (f32[8]{0:T(128)S(1)}, f32[8]{0:T(128)}, u32[]{:S(2)}) copy-start(f32[8]{0:T(128)} %temp_ref.1) | copy-start | bytes 100
  32.8 9.6 %collective-permute-start.7 = (f32[136,128]{1,0:T(8,128)S(1)}, f32[136,128]{1,0:T(8,128)S(1)}, u32[]{:S(2)}, u32[]{:S(2)}) collective-permute-start(f32[136,128]{1,0:T(8,128)S(1)} %add_add_fusion.1), channel_id=1, source_target_pairs={{0,64},{1,5},{2,66},{3,7},{4,68},{5,1},{6,70},{7,3},{8,72},{9,13},... | collective-permute-start | bytes 208904 | tf_op jit(solution)/shard_map/ppermute | solution.py:679
  37.6 4.9 %collective-permute-start.8 = (f32[136,128]{1,0:T(8,128)S(1)}, f32[136,128]{1,0:T(8,128)S(1)}, u32[]{:S(2)}, u32[]{:S(2)}) collective-permute-start(f32[136,128]{1,0:T(8,128)S(1)} %add_add_fusion.1), channel_id=1, source_target_pairs={{0,32},{1,3},{2,34},{3,1},{4,36},{5,7},{6,38},{7,5},{8,40},{9,11},... | collective-permute-start | bytes 208904 | tf_op jit(solution)/shard_map/ppermute | solution.py:679
  38.3 4.4 %collective-permute-start.9 = (f32[136,128]{1,0:T(8,128)S(1)}, f32[136,128]{1,0:T(8,128)S(1)}, u32[]{:S(2)}, u32[]{:S(2)}) collective-permute-start(f32[136,128]{1,0:T(8,128)S(1)} %add_add_fusion.1), channel_id=1, source_target_pairs={{0,96},{1,7},{2,98},{3,5},{4,100},{5,3},{6,102},{7,1},{8,104},{9,1... | collective-permute-start | bytes 208904 | tf_op jit(solution)/shard_map/ppermute | solution.py:679
  45.0 6.5 %collective-permute-start.10 = (f32[224,128]{1,0:T(8,128)S(1)}, f32[224,128]{1,0:T(8,128)S(1)}, u32[]{:S(2)}, u32[]{:S(2)}) collective-permute-start(f32[224,128]{1,0:T(8,128)S(1)} %middle.1.mine_ref), channel_id=1, source_target_pairs={{0,1},{1,0},{2,3},{3,2},{4,5},{5,4},{6,7},{7,6},{8,9},{9,8},{10,11... | collective-permute-start | bytes 344072 | tf_op jit(solution)/shard_map/ppermute | solution.py:683
  62.0 1.8 %collective-permute-start.11 = (bf16[704,256]{1,0:T(8,128)(2,1)S(1)}, bf16[704,256]{1,0:T(8,128)(2,1)S(1)}, u32[]{:S(2)}, u32[]{:S(2)}) collective-permute-start(bf16[704,256]{1,0:T(8,128)(2,1)S(1)} %get-tuple-element.57), channel_id=1, source_target_pairs={{0,1},{1,0},{2,3},{3,2},{4,5},{5,4},{6,7},{7,6},{8,9},{9,8},{10,11... | collective-permute-start | bytes 1081352 | tf_op jit(solution)/shard_map/ppermute | solution.py:683
  63.9 6.9 %collective-permute-start.12 = (bf16[176,256]{1,0:T(8,128)(2,1)S(1)}, bf16[176,256]{1,0:T(8,128)(2,1)S(1)}, u32[]{:S(2)}, u32[]{:S(2)}) collective-permute-start(bf16[176,256]{1,0:T(8,128)(2,1)S(1)} %get-tuple-element.59), channel_id=1, source_target_pairs={{0,2},{1,9},{2,0},{3,11},{4,6},{5,13},{6,4},{7,15},{8,10},{9,1},{1... | collective-permute-start | bytes 270344 | tf_op jit(solution)/shard_map/ppermute | solution.py:679
  64.0 6.8 %collective-permute-start.13 = (bf16[176,256]{1,0:T(8,128)(2,1)S(1)}, bf16[176,256]{1,0:T(8,128)(2,1)S(1)}, u32[]{:S(2)}, u32[]{:S(2)}) collective-permute-start(bf16[176,256]{1,0:T(8,128)(2,1)S(1)} %get-tuple-element.60), channel_id=1, source_target_pairs={{0,4},{1,17},{2,6},{3,19},{4,0},{5,21},{6,2},{7,23},{8,12},{9,25},... | collective-permute-start | bytes 270344 | tf_op jit(solution)/shard_map/ppermute | solution.py:679
  65.0 5.8 %collective-permute-start.14 = (bf16[176,256]{1,0:T(8,128)(2,1)S(1)}, bf16[176,256]{1,0:T(8,128)(2,1)S(1)}, u32[]{:S(2)}, u32[]{:S(2)}) collective-permute-start(bf16[176,256]{1,0:T(8,128)(2,1)S(1)} %get-tuple-element.61), channel_id=1, source_target_pairs={{0,6},{1,25},{2,4},{3,27},{4,2},{5,29},{6,0},{7,31},{8,14},{9,17},... | collective-permute-start | bytes 270344 | tf_op jit(solution)/shard_map/ppermute | solution.py:679
  70.9 6.3 %collective-permute-start.15 = (bf16[176,256]{1,0:T(8,128)(2,1)S(1)}, bf16[176,256]{1,0:T(8,128)(2,1)S(1)}, u32[]{:S(2)}, u32[]{:S(2)}) collective-permute-start(bf16[176,256]{1,0:T(8,128)(2,1)S(1)} %convert_element_type.39), channel_id=1, source_target_pairs={{0,16},{1,65},{2,18},{3,67},{4,20},{5,69},{6,22},{7,71},{8,24},{9,... | collective-permute-start | bytes 270344 | tf_op jit(solution)/shard_map/ppermute | solution.py:679
  71.0 6.2 %collective-permute-start.16 = (bf16[176,256]{1,0:T(8,128)(2,1)S(1)}, bf16[176,256]{1,0:T(8,128)(2,1)S(1)}, u32[]{:S(2)}, u32[]{:S(2)}) collective-permute-start(bf16[176,256]{1,0:T(8,128)(2,1)S(1)} %convert_element_type.39), channel_id=1, source_target_pairs={{0,8},{1,33},{2,10},{3,35},{4,12},{5,37},{6,14},{7,39},{8,0},{9,41... | collective-permute-start | bytes 270344 | tf_op jit(solution)/shard_map/ppermute | solution.py:679
  71.1 6.1 %collective-permute-start.17 = (bf16[176,256]{1,0:T(8,128)(2,1)S(1)}, bf16[176,256]{1,0:T(8,128)(2,1)S(1)}, u32[]{:S(2)}, u32[]{:S(2)}) collective-permute-start(bf16[176,256]{1,0:T(8,128)(2,1)S(1)} %convert_element_type.39), channel_id=1, source_target_pairs={{0,24},{1,97},{2,26},{3,99},{4,28},{5,101},{6,30},{7,103},{8,16},{... | collective-permute-start | bytes 270344 | tf_op jit(solution)/shard_map/ppermute | solution.py:679
  77.3 6.3 %collective-permute-start.18 = (bf16[176,256]{1,0:T(8,128)(2,1)S(1)}, bf16[176,256]{1,0:T(8,128)(2,1)S(1)}, u32[]{:S(2)}, u32[]{:S(2)}) collective-permute-start(bf16[176,256]{1,0:T(8,128)(2,1)S(1)} %convert_element_type.43), channel_id=1, source_target_pairs={{0,64},{1,5},{2,66},{3,7},{4,68},{5,1},{6,70},{7,3},{8,72},{9,13},... | collective-permute-start | bytes 270344 | tf_op jit(solution)/shard_map/ppermute | solution.py:679
  78.2 5.4 %collective-permute-start.19 = (bf16[176,256]{1,0:T(8,128)(2,1)S(1)}, bf16[176,256]{1,0:T(8,128)(2,1)S(1)}, u32[]{:S(2)}, u32[]{:S(2)}) collective-permute-start(bf16[176,256]{1,0:T(8,128)(2,1)S(1)} %convert_element_type.43), channel_id=1, source_target_pairs={{0,32},{1,3},{2,34},{3,1},{4,36},{5,7},{6,38},{7,5},{8,40},{9,11},... | collective-permute-start | bytes 270344 | tf_op jit(solution)/shard_map/ppermute | solution.py:679
  78.9 4.7 %collective-permute-start.20 = (bf16[176,256]{1,0:T(8,128)(2,1)S(1)}, bf16[176,256]{1,0:T(8,128)(2,1)S(1)}, u32[]{:S(2)}, u32[]{:S(2)}) collective-permute-start(bf16[176,256]{1,0:T(8,128)(2,1)S(1)} %convert_element_type.43), channel_id=1, source_target_pairs={{0,96},{1,7},{2,98},{3,5},{4,100},{5,3},{6,102},{7,1},{8,104},{9,1... | collective-permute-start | bytes 270344 | tf_op jit(solution)/shard_map/ppermute | solution.py:679
  83.7 6.9 %collective-permute-start.21 = (bf16[176,256]{1,0:T(8,128)(2,1)S(1)}, bf16[176,256]{1,0:T(8,128)(2,1)S(1)}, u32[]{:S(2)}, u32[]{:S(2)}) collective-permute-start(bf16[176,256]{1,0:T(8,128)(2,1)S(1)} %add_reduce-precision_fusion), channel_id=1, source_target_pairs={{0,2},{1,9},{2,0},{3,11},{4,6},{5,13},{6,4},{7,15},{8,10},{9,1},{1... | collective-permute-start | bytes 270344 | tf_op jit(solution)/shard_map/ppermute | solution.py:679
  83.8 6.8 %collective-permute-start.22 = (bf16[176,256]{1,0:T(8,128)(2,1)S(1)}, bf16[176,256]{1,0:T(8,128)(2,1)S(1)}, u32[]{:S(2)}, u32[]{:S(2)}) collective-permute-start(bf16[176,256]{1,0:T(8,128)(2,1)S(1)} %add_reduce-precision_fusion), channel_id=1, source_target_pairs={{0,4},{1,17},{2,6},{3,19},{4,0},{5,21},{6,2},{7,23},{8,12},{9,25},... | collective-permute-start | bytes 270344 | tf_op jit(solution)/shard_map/ppermute | solution.py:679
  86.7 4.6 %collective-permute-start.23 = (bf16[176,256]{1,0:T(8,128)(2,1)S(1)}, bf16[176,256]{1,0:T(8,128)(2,1)S(1)}, u32[]{:S(2)}, u32[]{:S(2)}) collective-permute-start(bf16[176,256]{1,0:T(8,128)(2,1)S(1)} %add_reduce-precision_fusion), channel_id=1, source_target_pairs={{0,6},{1,25},{2,4},{3,27},{4,2},{5,29},{6,0},{7,31},{8,14},{9,17},... | collective-permute-start | bytes 270344 | tf_op jit(solution)/shard_map/ppermute | solution.py:679
  91.4 6.7 %collective-permute-start.24 = (bf16[4,176,256]{2,1,0:T(8,128)(2,1)S(1)}, bf16[4,176,256]{2,1,0:T(8,128)(2,1)S(1)}, u32[]{:S(2)}, u32[]{:S(2)}) collective-permute-start(bf16[4,176,256]{2,1,0:T(8,128)(2,1)S(1)} %pad_maximum_fusion.mine_ref), channel_id=1, source_target_pairs={{0,1},{1,0},{2,3},{3,2},{4,5},{5,4},{6,7},{7,6},{8,9},{9,8},{10,11... | collective-permute-start | bytes 1081352 | tf_op jit(solution)/shard_map/ppermute | solution.py:683
